TPU v7x, 256 devices: a whole 4x4x8 slice. The times are simulated.
256 devices in a mesh: az: 32 (over y, x, z_lo), rad: 8 (over z_hi, core).
Axes of the slice: x: 4, y: 4, z: 8 (z_hi: 4, z_lo: 2; z = z_hi * 2 + z_lo), core: 2. Of those that a mesh axis runs over, the one named last changes fastest.
Arguments:
- state: float32 [8, 32, 64, 4096], P(None, 'rad', None, 'az'), may hold values from -6 to 6
- shifts: int32 [32], P('rad'), may hold values from 0 to 4095
- fracs: float32 [32], P('rad'), may hold values from 0 to 1
Outputs:
- advanced: float32 [8, 32, 64, 4096], P(None, 'rad', None, 'az')
All inputs are finite; a program needn't handle non-finite values.
Results may differ from a plain program's by a relative error of at most 0.00002.
Values sent between devices are 32-bit elements; how exact they have to be, the bound alone decides.
No kernel may reach another device: no remote copies, remote signals or barrier semaphores. Data moves between devices by JAX's collectives and lax.ppermute only.
A program may use at most 128 MiB of HBM per device.

v0:
```python
import jax
import jax.numpy as jnp
from jax import lax
from jax.sharding import PartitionSpec as P


def from_behind(value, axis, steps):
    count = lax.axis_size(axis)
    pairs = [(source, (source + steps) % count) for source in range(count)]
    return lax.ppermute(value, axis, pairs)


def with_halo(cells, sides, width, closed):
    for axis, dim in sides:
        count = lax.axis_size(axis)
        ends = count if closed else count - 1
        head = lax.slice_in_dim(cells, 0, width, axis=dim)
        tail = lax.slice_in_dim(cells, cells.shape[dim] - width, cells.shape[dim], axis=dim)
        cells = jnp.concatenate(
            [
                lax.ppermute(tail, axis, [(i, (i + 1) % count) for i in range(ends)]),
                cells,
                lax.ppermute(head, axis, [((i + 1) % count, i) for i in range(ends)]),
            ],
            axis=dim,
        )
    return cells


def fields(S):
    rho, vx, vy, vz, bx, by, bz, ent = [S[i] for i in range(8)]
    return jnp.stack(
        [
            vy * bz - vz * by,
            vz * bx - vx * bz,
            vx * by - vy * bx,
            rho * vx,
            rho * vy,
            rho * vz,
            ent,
            0.5 * (bx * bx + by * by + bz * bz),
        ]
    )


def advance(center, xplus, xminus, yplus, yminus, coord_x, coord_z):
    dxf = 0.5 * (fields(xplus) - fields(xminus))
    dyf = 0.5 * (fields(yplus) - fields(yminus))
    fc = fields(center)
    fpad = jnp.pad(fc, ((0, 0), (0, 0), (1, 1), (0, 0)))
    dzf = 0.5 * (fpad[:, :, 2:] - fpad[:, :, :-2])
    rho, vx, vy, vz, bx, by, bz, ent = [center[i] for i in range(8)]
    rates = jnp.stack(
        [
            -(dxf[3] + dyf[4] + dzf[5]),
            2.0 * vy + 3.0 * coord_x - dxf[7],
            -0.5 * vx - dyf[7],
            -coord_z - dzf[7],
            dyf[2] - dzf[1],
            dzf[0] - dxf[2],
            dxf[1] - dyf[0],
            -(vx * dxf[6] + vy * dyf[6] + vz * dzf[6]),
        ]
    )
    return center + 0.2 * rates


def interpolate(extended, starts, fracs, length):

    def cut_row(row, start):
        return lax.dynamic_slice_in_dim(row, start, length + 1, 2)

    pieces = jax.vmap(cut_row, in_axes=(1, 0), out_axes=1)(extended, starts)
    weight = fracs[None, :, None, None]
    return (1.0 - weight) * pieces[..., 1:] + weight * pieces[..., :-1]


def on_device(state, shifts, fracs):
    radii = state.shape[1]
    width = state.shape[3]
    blocks = shifts // width
    within = shifts % width
    current = state
    levels = lax.axis_size("az").bit_length() - 1
    for level in range(levels):
        moved = from_behind(current, "az", 1 << level)
        taken = blocks >> level & 1 == 1
        current = jnp.where(taken[None, :, None, None], moved, current)
    previous = from_behind(current, "az", 1)
    joined = jnp.concatenate([previous, current], axis=3)
    remapped = interpolate(joined, width - within - 1, fracs, width)
    padded_rad = with_halo(remapped, (("rad", 1),), 1, False)
    padded_az = with_halo(remapped, (("az", 3),), 1, True)
    total_radii = radii * lax.axis_size("rad")
    first = lax.axis_index("rad") * radii
    radius_index = (first + jnp.arange(radii, dtype=jnp.int32)).astype(jnp.float32)
    coord_x = ((radius_index + 0.5) / total_radii - 0.5)[:, None, None]
    heights = state.shape[2]
    coord_z = ((jnp.arange(heights, dtype=jnp.float32) + 0.5) / heights - 0.5)[None, :, None]
    return advance(
        remapped,
        padded_rad[:, 2:],
        padded_rad[:, :-2],
        padded_az[..., 2:],
        padded_az[..., :-2],
        coord_x,
        coord_z,
    )


def solution(mesh):
    in_specs = (P(None, "rad", None, "az"), P("rad"), P("rad"))
    out_specs = P(None, "rad", None, "az")
    return jax.shard_map(
        on_device, mesh=mesh, in_specs=in_specs, out_specs=out_specs, check_vma=False
    )
```

profile of v0, /device:TPU:1, one launch (start us, length us, event | category | flops | bytes accessed | tf_op | source)
XLA Modules:
  0.0 253.6 jit_solution(3086971571594779999)
XLA Ops:
  2.5 4.1 %copy.34 = f32[8,4,64,128]{2,0,1,3:T(8,128)} copy(f32[8,4,64,128]{3,2,1,0:T(8,128)} %param.3) | data formatting | bytes 2097152 | tf_op args[0]
  6.6 22.1 %collective-permute-done = f32[8,4,64,128]{3,2,1,0:T(8,128)S(1)} collective-permute-done((f32[8,4,64,128]{3,2,1,0:T(8,128)}, f32[8,4,64,128]{3,2,1,0:T(8,128)S(1)}, u32[]{:S(2)}, u32[]{:S(2)}) %collective-permute-start) | collective-permute-done | bytes 1048608 | tf_op jit(solution)/shard_map/ppermute | solution.py:10
  28.7 2.9 %copy.33 = f32[8,4,64,128]{2,0,1,3:T(8,128)} copy(f32[8,4,64,128]{3,2,1,0:T(8,128)S(1)} %collective-permute-done) | data formatting | bytes 2097152 | tf_op jit(solution)/shard_map/ppermute | solution.py:10
  31.6 2.7 %broadcast_select_fusion = f32[8,4,64,128]{2,0,1,3:T(8,128)S(1)} fusion(f32[8,4,64,128]{2,0,1,3:T(8,128)} %copy.33, f32[8,4,64,128]{2,0,1,3:T(8,128)} %copy.34, pred[4]{0:T(512)(128)(4,1)S(1)} %get-tuple-element.83), kind=kLoop, calls=%fused_computation.12 | loop fusion | flops 262144 | bytes 3145732 | tf_op jit(solution)/shard_map/jit(_where)/select_n | solution.py:88
  36.6 25.4 %collective-permute-done.1 = f32[8,4,64,128]{3,2,1,0:T(8,128)S(1)} collective-permute-done((f32[8,4,64,128]{3,2,1,0:T(8,128)}, f32[8,4,64,128]{3,2,1,0:T(8,128)S(1)}, u32[]{:S(2)}, u32[]{:S(2)}) %collective-permute-start.1) | collective-permute-done | bytes 1048608 | tf_op jit(solution)/shard_map/ppermute | solution.py:10
  62.0 2.8 %copy.36 = f32[8,4,64,128]{2,0,1,3:T(8,128)} copy(f32[8,4,64,128]{3,2,1,0:T(8,128)S(1)} %collective-permute-done.1) | data formatting | bytes 2097152 | tf_op jit(solution)/shard_map/ppermute | solution.py:10
  64.8 3.4 %broadcast_select_fusion.1 = f32[8,4,64,128]{2,0,1,3:T(8,128)} fusion(f32[8,4,64,128]{2,0,1,3:T(8,128)} %copy.36, f32[8,4,64,128]{2,0,1,3:T(8,128)S(1)} %broadcast_select_fusion, pred[4]{0:T(512)(128)(4,1)S(1)} %get-tuple-element.81), kind=kLoop, calls=%fused_computation.13 | loop fusion | flops 262144 | bytes 3145732 | tf_op jit(solution)/shard_map/jit(_where)/select_n | solution.py:88
  71.2 24.6 %collective-permute-done.2 = f32[8,4,64,128]{3,2,1,0:T(8,128)S(1)} collective-permute-done((f32[8,4,64,128]{3,2,1,0:T(8,128)S(1)}, f32[8,4,64,128]{3,2,1,0:T(8,128)S(1)}, u32[]{:S(2)}, u32[]{:S(2)}) %collective-permute-start.2) | collective-permute-done | bytes 1048608 | tf_op jit(solution)/shard_map/ppermute | solution.py:10
  95.8 2.9 %copy.38 = f32[8,4,64,128]{2,0,1,3:T(8,128)} copy(f32[8,4,64,128]{3,2,1,0:T(8,128)S(1)} %collective-permute-done.2) | data formatting | bytes 2097152 | tf_op jit(solution)/shard_map/ppermute | solution.py:10
  104.3 20.9 %collective-permute-done.3 = f32[8,4,64,128]{3,2,1,0:T(8,128)S(1)} collective-permute-done((f32[8,4,64,128]{3,2,1,0:T(8,128)}, f32[8,4,64,128]{3,2,1,0:T(8,128)S(1)}, u32[]{:S(2)}, u32[]{:S(2)}) %collective-permute-start.3) | collective-permute-done | bytes 1048608 | tf_op jit(solution)/shard_map/ppermute | solution.py:10
  125.2 2.8 %copy.40 = f32[8,4,64,128]{2,0,1,3:T(8,128)} copy(f32[8,4,64,128]{3,2,1,0:T(8,128)S(1)} %collective-permute-done.3) | data formatting | bytes 2097152 | tf_op jit(solution)/shard_map/ppermute | solution.py:10
  128.0 3.4 %broadcast_select_fusion.3 = f32[8,4,64,128]{2,0,1,3:T(8,128)} fusion(f32[8,4,64,128]{2,0,1,3:T(8,128)} %copy.40, f32[8,4,64,128]{2,0,1,3:T(8,128)S(1)} %broadcast_select_fusion.2, pred[4]{0:T(512)(128)(4,1)S(1)} %get-tuple-element.80), kind=kLoop, calls=%fused_computation.15 | loop fusion | flops 262144 | bytes 3145732 | tf_op jit(solution)/shard_map/jit(_where)/select_n | solution.py:88
  131.4 3.6 %copy.41 = f32[8,4,64,128]{3,2,1,0:T(8,128)} copy(f32[8,4,64,128]{2,0,1,3:T(8,128)} %broadcast_select_fusion.3) | data formatting | bytes 2097152 | tf_op jit(solution)/shard_map/jit(_where)/select_n | solution.py:88
  137.3 18.7 %collective-permute-done.4 = f32[8,4,64,128]{3,2,1,0:T(8,128)S(1)} collective-permute-done((f32[8,4,64,128]{3,2,1,0:T(8,128)}, f32[8,4,64,128]{3,2,1,0:T(8,128)S(1)}, u32[]{:S(2)}, u32[]{:S(2)}) %collective-permute-start.4) | collective-permute-done | bytes 1048608 | tf_op jit(solution)/shard_map/ppermute | solution.py:10
  155.9 2.9 %copy.42 = f32[8,4,64,128]{2,0,1,3:T(8,128)} copy(f32[8,4,64,128]{3,2,1,0:T(8,128)S(1)} %collective-permute-done.4) | data formatting | bytes 2097152 | tf_op jit(solution)/shard_map/ppermute | solution.py:10
  158.8 3.5 %broadcast_select_fusion.4 = f32[8,4,64,128]{2,0,1,3:T(8,128)} fusion(f32[8,4,64,128]{2,0,1,3:T(8,128)} %copy.42, f32[8,4,64,128]{2,0,1,3:T(8,128)S(1)} %copy-done, pred[4]{0:T(512)(128)(4,1)S(1)} %get-tuple-element.45), kind=kLoop, calls=%fused_computation.16 | loop fusion | flops 262144 | bytes 3145732 | tf_op jit(solution)/shard_map/jit(_where)/select_n | solution.py:88
  162.3 3.6 %copy.43 = f32[8,4,64,128]{3,2,1,0:T(8,128)} copy(f32[8,4,64,128]{2,0,1,3:T(8,128)} %broadcast_select_fusion.4) | data formatting | bytes 2097152 | tf_op jit(solution)/shard_map/jit(_where)/select_n | solution.py:88
  165.9 3.5 %collective-permute-start.5 = (f32[8,4,64,128]{3,2,1,0:T(8,128)}, f32[8,4,64,128]{3,2,1,0:T(8,128)S(1)}, u32[]{:S(2)}, u32[]{:S(2)}) collective-permute-start(f32[8,4,64,128]{3,2,1,0:T(8,128)} %copy.43), channel_id=1, source_target_pairs={{0,8},{8,16},{16,24},{24,32},{32,40},{40,48},{48,56},{56,64},{64,7... | collective-permute-start | bytes 3145736 | tf_op jit(solution)/shard_map/ppermute | solution.py:10
  170.6 18.0 %collective-permute-done.5 = f32[8,4,64,128]{3,2,1,0:T(8,128)S(1)} collective-permute-done((f32[8,4,64,128]{3,2,1,0:T(8,128)}, f32[8,4,64,128]{3,2,1,0:T(8,128)S(1)}, u32[]{:S(2)}, u32[]{:S(2)}) %collective-permute-start.5) | collective-permute-done | bytes 1048608 | tf_op jit(solution)/shard_map/ppermute | solution.py:10
  188.6 2.9 %copy.44 = f32[8,4,64,128]{2,0,1,3:T(8,128)} copy(f32[8,4,64,128]{3,2,1,0:T(8,128)S(1)} %collective-permute-done.5) | data formatting | bytes 2097152 | tf_op jit(solution)/shard_map/ppermute | solution.py:10
  191.5 4.1 %maximum_bitcast_fusion = f32[4,8,64,256]{2,1,0,3:T(8,128)} fusion(f32[8,4,64,128]{2,0,1,3:T(8,128)S(1)} %copy-done.3, f32[8,4,64,128]{2,0,1,3:T(8,128)} %copy.44), kind=kLoop, calls=%fused_computation.1 | loop fusion | flops 524288 | bytes 4194304 | tf_op jit(solution)/shard_map/vmap()/transpose | solution.py:71
  195.5 4.4 %gather_fusion = f32[4,8,64,129]{2,1,3,0:T(8,128)} fusion(f32[4,8,64,256]{2,1,0,3:T(8,128)} %maximum_bitcast_fusion, s32[4]{0:T(128)S(1)} %fusion.20), kind=kCustom, calls=%fused_computation | custom fusion | bytes 2113600 | tf_op jit(solution)/shard_map/vmap()/gather | solution.py:71
  207.6 19.1 %collective-permute-start.7 = (f32[8,1,64,128]{3,2,1,0:T(8,128)}, f32[8,1,64,128]{3,2,1,0:T(8,128)S(1)}, u32[]{:S(2)}, u32[]{:S(2)}) collective-permute-start(f32[8,1,64,128]{3,2,1,0:T(8,128)} %get-tuple-element.71), channel_id=1, source_target_pairs={{0,1},{1,2},{2,3},{3,4},{4,5},{5,6},{6,7},{8,9},{9,10},{10,11},{11... | collective-permute-start | bytes 786440 | tf_op jit(solution)/shard_map/ppermute | solution.py:21
  229.0 6.0 %collective-permute-start.8 = (f32[8,4,64,1]{2,0,3,1:T(8,128)S(1)}, f32[8,4,64,1]{2,0,3,1:T(8,128)S(1)}, u32[]{:S(2)}, u32[]{:S(2)}) collective-permute-start(f32[8,4,64,1]{2,0,3,1:T(8,128)S(1)} %copy.46), channel_id=1, source_target_pairs={{8,0},{16,8},{24,16},{32,24},{40,32},{48,40},{56,48},{64,56},{72,6... | collective-permute-start | bytes 24584 | tf_op jit(solution)/shard_map/ppermute | solution.py:23
  (106 shorter events, 44.9 us)
Async XLA Ops:
  0.0 6.5 %copy-start.19 = (s32[4]{0:T(128)S(1)}, s32[4]{0:T(128)}, u32[]{:S(2)}) copy-start(s32[4]{0:T(128)} %param.4) | copy-start | bytes 52
  0.0 28.7 %collective-permute-start = (f32[8,4,64,128]{3,2,1,0:T(8,128)}, f32[8,4,64,128]{3,2,1,0:T(8,128)S(1)}, u32[]{:S(2)}, u32[]{:S(2)}) collective-permute-start(f32[8,4,64,128]{3,2,1,0:T(8,128)} %param.3), channel_id=1, source_target_pairs={{0,8},{8,16},{16,24},{24,32},{32,40},{40,48},{48,56},{56,64},{64,7... | collective-permute-start | bytes 3145736 | tf_op jit(solution)/shard_map/ppermute | solution.py:10
  36.6 25.5 %collective-permute-start.1 = (f32[8,4,64,128]{3,2,1,0:T(8,128)}, f32[8,4,64,128]{3,2,1,0:T(8,128)S(1)}, u32[]{:S(2)}, u32[]{:S(2)}) collective-permute-start(f32[8,4,64,128]{3,2,1,0:T(8,128)} %copy.35), channel_id=1, source_target_pairs={{0,16},{8,24},{16,32},{24,40},{32,48},{40,56},{48,64},{56,72},{64,... | collective-permute-start | bytes 3145736 | tf_op jit(solution)/shard_map/ppermute | solution.py:10
  70.9 24.9 %collective-permute-start.2 = (f32[8,4,64,128]{3,2,1,0:T(8,128)S(1)}, f32[8,4,64,128]{3,2,1,0:T(8,128)S(1)}, u32[]{:S(2)}, u32[]{:S(2)}) collective-permute-start(f32[8,4,64,128]{3,2,1,0:T(8,128)S(1)} %copy.37), channel_id=1, source_target_pairs={{0,32},{8,40},{16,48},{24,56},{32,64},{40,72},{48,80},{56,88},{64,... | collective-permute-start | bytes 3145736 | tf_op jit(solution)/shard_map/ppermute | solution.py:10
  103.7 21.5 %collective-permute-start.3 = (f32[8,4,64,128]{3,2,1,0:T(8,128)}, f32[8,4,64,128]{3,2,1,0:T(8,128)S(1)}, u32[]{:S(2)}, u32[]{:S(2)}) collective-permute-start(f32[8,4,64,128]{3,2,1,0:T(8,128)} %copy.39), channel_id=1, source_target_pairs={{0,64},{8,72},{16,80},{24,88},{32,96},{40,104},{48,112},{56,120},{... | collective-permute-start | bytes 3145736 | tf_op jit(solution)/shard_map/ppermute | solution.py:10
  135.1 23.7 %copy-start = (f32[8,4,64,128]{2,0,1,3:T(8,128)S(1)}, f32[8,4,64,128]{2,0,1,3:T(8,128)}, u32[]{:S(2)}) copy-start(f32[8,4,64,128]{2,0,1,3:T(8,128)} %broadcast_select_fusion.3) | copy-start | bytes 3145732
  135.1 20.9 %collective-permute-start.4 = (f32[8,4,64,128]{3,2,1,0:T(8,128)}, f32[8,4,64,128]{3,2,1,0:T(8,128)S(1)}, u32[]{:S(2)}, u32[]{:S(2)}) collective-permute-start(f32[8,4,64,128]{3,2,1,0:T(8,128)} %copy.41), channel_id=1, source_target_pairs={{0,128},{8,136},{16,144},{24,152},{32,160},{40,168},{48,176},{56,1... | collective-permute-start | bytes 3145736 | tf_op jit(solution)/shard_map/ppermute | solution.py:10
  162.3 8.3 %copy-start.13 = (f32[4]{0:T(128)S(1)}, f32[4]{0:T(128)}, u32[]{:S(2)}) copy-start(f32[4]{0:T(128)} %param.5) | copy-start | bytes 52
  165.9 25.5 %copy-start.3 = (f32[8,4,64,128]{2,0,1,3:T(8,128)S(1)}, f32[8,4,64,128]{2,0,1,3:T(8,128)}, u32[]{:S(2)}) copy-start(f32[8,4,64,128]{2,0,1,3:T(8,128)} %broadcast_select_fusion.4) | copy-start | bytes 3145732
  165.9 22.7 %collective-permute-start.5 = (f32[8,4,64,128]{3,2,1,0:T(8,128)}, f32[8,4,64,128]{3,2,1,0:T(8,128)S(1)}, u32[]{:S(2)}, u32[]{:S(2)}) collective-permute-start(f32[8,4,64,128]{3,2,1,0:T(8,128)} %copy.43), channel_id=1, source_target_pairs={{0,8},{8,16},{16,24},{24,32},{32,40},{40,48},{48,56},{56,64},{64,7... | collective-permute-start | bytes 3145736 | tf_op jit(solution)/shard_map/ppermute | solution.py:10
  170.6 31.8 %copy-start.15 = (f32[4]{0:T(128)}, f32[4]{0:T(128)S(1)}, u32[]{:S(2)}) copy-start(f32[4]{0:T(128)S(1)} %broadcast_subtract_fusion) | copy-start | bytes 52
  202.4 2.1 copy-start.1
  204.4 24.1 %copy-start.4 = (f32[8,4,64,1]{3,2,1,0:T(8,128)S(1)}, f32[8,4,64,1]{3,2,1,0:T(8,128)}, u32[]{:S(2)}) copy-start(f32[8,4,64,1]{3,2,1,0:T(8,128)} %get-tuple-element.79) | copy-start | bytes 24580
  206.1 28.8 %collective-permute-start.9 = (f32[8,4,64,1]{2,0,3,1:T(8,128)S(1)}, f32[8,4,64,1]{2,0,3,1:T(8,128)S(1)}, u32[]{:S(2)}, u32[]{:S(2)}) collective-permute-start(f32[8,4,64,1]{2,0,3,1:T(8,128)S(1)} %copy.48), channel_id=1, source_target_pairs={{0,8},{8,16},{16,24},{24,32},{32,40},{40,48},{48,56},{56,64},{64,7... | collective-permute-start | bytes 24584 | tf_op jit(solution)/shard_map/ppermute | solution.py:21
  207.6 31.9 %collective-permute-start.7 = (f32[8,1,64,128]{3,2,1,0:T(8,128)}, f32[8,1,64,128]{3,2,1,0:T(8,128)S(1)}, u32[]{:S(2)}, u32[]{:S(2)}) collective-permute-start(f32[8,1,64,128]{3,2,1,0:T(8,128)} %get-tuple-element.71), channel_id=1, source_target_pairs={{0,1},{1,2},{2,3},{3,4},{4,5},{5,6},{6,7},{8,9},{9,10},{10,11},{11... | collective-permute-start | bytes 786440 | tf_op jit(solution)/shard_map/ppermute | solution.py:21
  226.7 12.8 %collective-permute-start.6 = (f32[8,1,64,128]{3,2,1,0:T(8,128)}, f32[8,1,64,128]{3,2,1,0:T(8,128)}, u32[]{:S(2)}, u32[]{:S(2)}) collective-permute-start(f32[8,1,64,128]{3,2,1,0:T(8,128)} %get-tuple-element.72), channel_id=1, source_target_pairs={{1,0},{2,1},{3,2},{4,3},{5,4},{6,5},{7,6},{9,8},{10,9},{11,10},{12... | collective-permute-start | bytes 786440 | tf_op jit(solution)/shard_map/ppermute | solution.py:23
  229.0 8.3 %collective-permute-start.8 = (f32[8,4,64,1]{2,0,3,1:T(8,128)S(1)}, f32[8,4,64,1]{2,0,3,1:T(8,128)S(1)}, u32[]{:S(2)}, u32[]{:S(2)}) collective-permute-start(f32[8,4,64,1]{2,0,3,1:T(8,128)S(1)} %copy.46), channel_id=1, source_target_pairs={{8,0},{16,8},{24,16},{32,24},{40,32},{48,40},{56,48},{64,56},{72,6... | collective-permute-start | bytes 24584 | tf_op jit(solution)/shard_map/ppermute | solution.py:23
  242.6 2.0 copy-start.5
  242.6 2.0 copy-start.10
  249.1 1.0 copy-start.7
  249.1 1.0 copy-start.12
  250.6 1.6 copy-start.2
  250.7 1.6 copy-start.14
  250.7 1.6 copy-start.16
  (6 other events, 5.1 us)
where the time goes:
time: 254 us
  waiting for transfers between devices  130 us (51%)
  local copies, waits for them, and re-layouts  49.9 us (20%)
  other arithmetic  36.9 us (15%)
  starting transfers between devices  36.7 us (14%)
    ppermute x6, waiting for transfers between devices, from_behind(): return lax.ppermute(value, axis, pairs)  130 us
    ppermute x2, starting transfers between devices, with_halo(): lax.ppermute(tail, axis, [(i, (i + 1) % count) for i in range(ends)])  19.7 us
    ppermute x6, local copies, waits for them, and re-layouts, from_behind(): return lax.ppermute(value, axis, pairs)  17.1 us
    select_n x5, other arithmetic, on_device(): current = jnp.where(taken[None, :, None, None], moved, current)  15.9 us
    select_n x5, local copies, waits for them, and re-layouts, on_device(): current = jnp.where(taken[None, :, None, None], moved, current)  14.4 us
    unnamed x28, other arithmetic  11.7 us
    ppermute x6, starting transfers between devices, from_behind(): return lax.ppermute(value, axis, pairs)  9.02 us
    ppermute x2, starting transfers between devices, with_halo(): lax.ppermute(head, axis, [((i + 1) % count, i) for i in range(ends)])  7.93 us
  transfers between devices with their start and end apart: 10, of which 6 were waited for; matrix products, arithmetic and copies ran while one was open for 4% of the time, Pallas kernels for 0%

commit v1 on v0

v1 whole, which is shorter than its diff:
```python
import jax
import jax.numpy as jnp
from jax import lax
from jax.experimental import pallas as pl
from jax.experimental.pallas import tpu as pltpu
from jax.sharding import PartitionSpec as P

F32 = jnp.float32
VMEM = pl.BlockSpec(memory_space=pltpu.VMEM)
SMEM = pl.BlockSpec(memory_space=pltpu.SMEM)


def remap_kernel(steps_ref, frac_ref, x_ref, o_ref):
    blocks, height, width = x_ref.shape
    block_shift = steps_ref[0]
    lane_shift = steps_ref[1]
    frac = frac_ref[0]
    lane = lax.broadcasted_iota(jnp.int32, (height, width), 1)
    own = lane + lane_shift < width
    own_next = lane + lane_shift + 1 < width
    ends = jnp.zeros((height, width), F32)
    for i in range(blocks):
        near = x_ref[lax.rem(i - block_shift + 2 * blocks, blocks)]
        far = x_ref[lax.rem(i - block_shift - 1 + 2 * blocks, blocks)]
        first = pltpu.roll(jnp.where(own, near, far), lane_shift, 1)
        second = pltpu.roll(jnp.where(own_next, near, far), lane_shift + 1, 1)
        cells = (1.0 - frac) * first + frac * second
        o_ref[i, :height, :] = cells
        turned = pltpu.roll(cells, (2 * i + 1) % width, 1)
        ends = jnp.where(lane // 2 == i, turned, ends)
    rows = jnp.transpose(jnp.concatenate([ends, jnp.zeros_like(ends)], axis=0))
    for i in range(blocks):
        last = 2 * ((i - 1) % blocks)
        head = 2 * ((i + 1) % blocks) + 1
        o_ref[i, height : height + 1, :] = rows[last : last + 1]
        o_ref[i, height + 1 : height + 2, :] = rows[head : head + 1]


def products(S):
    rho, vx, vy, vz, bx, by, bz, ent = S
    return (
        vy * bz - vz * by,
        vz * bx - vx * bz,
        vx * by - vy * bx,
        rho * vx,
        rho * vy,
        rho * vz,
        ent,
        0.5 * (bx * bx + by * by + bz * bz),
    )


def edge_kernel(s_ref, low_ref, high_ref):
    radii = s_ref.shape[1]
    height = low_ref.shape[1]
    for r, out in ((0, low_ref), (radii - 1, high_ref)):
        wx, wy, wz, fx, fy, fz, es, pm = products([s_ref[v, r, :height] for v in range(8)])
        for at, field in enumerate((wy, wz, fx, es, pm)):
            out[at] = field


def update_kernel(first_ref, s_ref, below_ref, above_ref, o_ref, f_ref):
    radii = s_ref.shape[1]
    height, width = o_ref.shape[2:]
    total_radii = first_ref[1]
    pad = 8
    lane = lax.broadcasted_iota(jnp.int32, (height, width), 1)
    level = lax.broadcasted_iota(jnp.int32, (height, width), 0)
    zk = (level.astype(F32) + 0.5) / height - 0.5
    for r in range(radii):
        for at, field in enumerate(products([s_ref[v, r, :height] for v in range(8)])):
            f_ref[at, r, pad : pad + height] = field
            f_ref[at, r, :pad] = jnp.zeros((pad, width), F32)
            f_ref[at, r, pad + height :] = jnp.zeros((pad, width), F32)
    sides = [
        jnp.concatenate([s_ref[v, r, height : height + 2] for r in range(radii)], axis=0)
        for v in range(8)
    ]
    wx, wy, wz, fx, fy, fz, es, pm = products(sides)
    rows = jnp.concatenate([wx, wz, fy, es, pm], axis=0)
    used = rows.shape[0]
    columns = jnp.transpose(
        jnp.concatenate([rows, jnp.zeros((width - used, width), F32)], axis=0)
    )[:height]
    spot = {0: 0, 2: 1, 4: 2, 6: 3, 7: 4}

    for r in range(radii):
        rho, vx, vy, vz, bx, by, bz, ent = [s_ref[v, r, :height] for v in range(8)]
        xr = ((first_ref[0] + r).astype(F32) + 0.5) / total_radii.astype(F32) - 0.5
        place = {1: 0, 2: 1, 3: 2, 6: 3, 7: 4}

        def dx(at):
            plus = above_ref[place[at]] if r == radii - 1 else f_ref[at, r + 1, pad : pad + height]
            minus = below_ref[place[at]] if r == 0 else f_ref[at, r - 1, pad : pad + height]
            return 0.5 * (plus - minus)

        def dy(at):
            here = f_ref[at, r, pad : pad + height]
            col = spot[at] * 2 * radii + 2 * r
            left = columns[:, col : col + 1]
            right = columns[:, col + 1 : col + 2]
            plus = jnp.where(lane == width - 1, right, pltpu.roll(here, width - 1, 1))
            minus = jnp.where(lane == 0, left, pltpu.roll(here, 1, 1))
            return 0.5 * (plus - minus)

        def dz(at):
            plus = f_ref[at, r, pad + 1 : pad + 1 + height]
            minus = f_ref[at, r, pad - 1 : pad - 1 + height]
            return 0.5 * (plus - minus)

        o_ref[0, r] = rho + 0.2 * -(dx(3) + dy(4) + dz(5))
        o_ref[1, r] = vx + 0.2 * (2.0 * vy + 3.0 * xr - dx(7))
        o_ref[2, r] = vy + 0.2 * (-0.5 * vx - dy(7))
        o_ref[3, r] = vz + 0.2 * (-zk - dz(7))
        o_ref[4, r] = bx + 0.2 * (dy(2) - dz(1))
        o_ref[5, r] = by + 0.2 * (dz(0) - dx(2))
        o_ref[6, r] = bz + 0.2 * (dx(1) - dy(0))
        o_ref[7, r] = ent + 0.2 * -(vx * dx(6) + vy * dy(6) + vz * dz(6))


def on_device(state, shifts, fracs):
    variables, radii, height, width = state.shape
    count = variables * radii
    bands = lax.axis_size("rad")
    band = lax.axis_index("rad")
    turned = lax.all_to_all(state.reshape(count, height, width), "az", 0, 0, tiled=True)
    mine = lax.axis_index("az") % radii
    shift = lax.dynamic_index_in_dim(shifts, mine, keepdims=False)
    frac = lax.dynamic_slice_in_dim(fracs, mine, 1)
    steps = jnp.stack([shift // width, shift % width])
    moved = pl.pallas_call(
        remap_kernel,
        out_shape=jax.ShapeDtypeStruct((count, height + 8, width), F32),
        in_specs=[SMEM, SMEM, VMEM],
        out_specs=VMEM,
        name="remap",
    )(steps, frac, turned)
    remapped = lax.all_to_all(moved, "az", 0, 0, tiled=True).reshape(
        variables, radii, height + 8, width
    )
    edge = jax.ShapeDtypeStruct((5, height, width), F32)
    low, high = pl.pallas_call(
        edge_kernel, out_shape=(edge, edge), in_specs=[VMEM], out_specs=(VMEM, VMEM), name="edges"
    )(remapped)
    below = lax.ppermute(high, "rad", [(i, i + 1) for i in range(bands - 1)])
    above = lax.ppermute(low, "rad", [(i + 1, i) for i in range(bands - 1)])
    places = jnp.stack([band * radii, bands * radii]).astype(jnp.int32)
    return pl.pallas_call(
        update_kernel,
        out_shape=jax.ShapeDtypeStruct(state.shape, F32),
        in_specs=[SMEM, VMEM, VMEM, VMEM],
        out_specs=VMEM,
        scratch_shapes=[pltpu.VMEM((8, radii, height + 16, width), F32)],
        compiler_params=pltpu.CompilerParams(vmem_limit_bytes=32 * 2**20),
        name="update",
    )(places, remapped, below, above)


def solution(mesh):
    in_specs = (P(None, "rad", None, "az"), P("rad"), P("rad"))
    out_specs = P(None, "rad", None, "az")
    return jax.shard_map(
        on_device, mesh=mesh, in_specs=in_specs, out_specs=out_specs, check_vma=False
    )
```

time: 254 us -> 77.3 us (0.30)
  waiting for transfers between devices: 130 us -> 19.7 us
  local copies, waits for them, and re-layouts: 49.9 us -> 2.22 us
  other arithmetic: 36.9 us -> 0.71 us
  blocking collectives: 0 us -> 21.7 us
  starting transfers between devices: 36.7 us -> 19.2 us
  Pallas kernels: 0 us -> 10.1 us
    ppermute x10 -> x2, waiting for transfers between devices: 130 us -> 7.49 us  [the longest x1 6.9 us: on_device(): above = lax.ppermute(low, 'rad', [(i + 1, i) for i in range(bands - 1)])]
    ppermute x10 -> x2, starting transfers between devices: 36.7 us -> 9.9 us  [the longest x1 7.98 us: on_device(): below = lax.ppermute(high, 'rad', [(i, i + 1) for i in range(bands - 1)])]
    all_to_all x0 -> x1, blocking collectives: none -> 21.7 us  [on_device(): lax.all_to_all(moved, 'az', 0, 0, tiled=True)]
    ppermute x8 -> x0, local copies, waits for them, and re-layouts: 17.9 us -> none  [the longest x6 17.1 us: from_behind(): return lax.ppermute(value, axis, pairs)]
    select_n x5 -> x0, other arithmetic: 15.9 us -> none  [on_device(): current = jnp.where(taken[None, :, None, None], moved, current)]
    select_n x5 -> x0, local copies, waits for them, and re-layouts: 14.4 us -> none  [on_device(): current = jnp.where(taken[None, :, None, None], moved, current)]
    all_to_all x0 -> x1, waiting for transfers between devices: none -> 12.2 us  [on_device(): lax.all_to_all(state.reshape(count, height, width), 'az', 0, 0, tiled=True)]
    unnamed x28 -> x0, other arithmetic: 11.7 us -> none
  transfers between devices with their start and end apart: 10 -> 3, of which waited for: 6 -> 3; matrix products, arithmetic and copies ran while one was open for 4% -> 3% of each run, Pallas kernels for 0% -> 0%
where the time goes in v1:
time: 77.3 us; the launch traced here: 76.3 us
  blocking collectives  21.7 us (28%)
  waiting for transfers between devices  19.7 us (25%)
  starting transfers between devices  19.2 us (25%)
  Pallas kernels  10.1 us (13%)
  between operations  2.67 us (3%)
  local copies, waits for them, and re-layouts  2.22 us (3%)
    all_to_all x1, blocking collectives, on_device(): lax.all_to_all(moved, 'az', 0, 0, tiled=True)  21.7 us
    all_to_all x1, waiting for transfers between devices, on_device(): lax.all_to_all(state.reshape(count, height, width), 'az', 0, 0, tiled=True)  12.2 us
    all_to_all x1, starting transfers between devices, on_device(): lax.all_to_all(state.reshape(count, height, width), 'az', 0, 0, tiled=True)  9.35 us
    ppermute x1, starting transfers between devices, on_device(): below = lax.ppermute(high, 'rad', [(i, i + 1) for i in range(bands - 1)])  7.98 us
    ppermute x1, waiting for transfers between devices, on_device(): above = lax.ppermute(low, 'rad', [(i + 1, i) for i in range(bands - 1)])  6.9 us
    pallas_call x1, Pallas kernels, on_device(): pl.pallas_call(remap_kernel, out_shape=jax.ShapeDtypeStruct((count, heigh...  5.51 us
    pallas_call x1, Pallas kernels, on_device(): pl.pallas_call(update_kernel, out_shape=jax.ShapeDtypeStruct(state.shape,...  2.49 us
    pallas_call x1, Pallas kernels, on_device(): pl.pallas_call(edge_kernel, out_shape=(edge, edge), in_specs=[VMEM], out_...  2.12 us
  transfers between devices with their start and end apart: 3, of which 3 were waited for; matrix products, arithmetic and copies ran while one was open for 3% of the time, Pallas kernels for 0%

profile of v1, /device:TPU:1, one launch (start us, length us, event | category | flops | bytes accessed | tf_op | source)
XLA Modules:
  0.0 76.3 jit_solution(7740641776512309018)
XLA Ops:
  0.0 0.0 copy-start.2
  0.0 0.0 copy-start.3
  0.0 9.4 %all-to-all-start = ((f32[32,64,128]{2,1,0:T(8,128)}), f32[32,64,128]{2,1,0:T(8,128)S(1)}, u32[]{:S(2)}, u32[]{:S(2)}) async-start(f32[32,64,128]{2,1,0:T(8,128)} %bitcast.8), calls=%async_computation | async-start | bytes 2097152 | tf_op jit(solution)/shard_map/all_to_all | solution.py:126
  9.4 0.0 copy-done.2
  9.4 0.6 dynamic_slice.7
  12.6 0.0 copy-done.3
  12.6 0.7 dynamic_slice.8.frac_ref
  13.3 0.6 pad_add_fusion.1.steps_ref
  13.9 12.2 %all-to-all-done.x_ref = f32[32,64,128]{2,1,0:T(8,128)S(1)} async-done(((f32[32,64,128]{2,1,0:T(8,128)}), f32[32,64,128]{2,1,0:T(8,128)S(1)}, u32[]{:S(2)}, u32[]{:S(2)}) %all-to-all-start) | async-done | bytes 1048608 | tf_op jit(solution)/shard_map/all_to_all | solution.py:126
  26.1 0.0 copy-start.1
  26.1 1.0 %copy-done.1 = f32[32,64,128]{2,1,0:T(8,128)} copy-done((f32[32,64,128]{2,1,0:T(8,128)}, f32[32,64,128]{2,1,0:T(8,128)S(1)}, u32[]{:S(2)}) %copy-start.1) | copy-done | bytes 1048600
  27.1 5.5 %remap.1 = f32[32,72,128]{2,1,0:T(8,128)} custom-call(s32[2]{0:T(128)} %pad_add_fusion.1.steps_ref, f32[1]{0:T(128)} %dynamic_slice.8.frac_ref, f32[32,64,128]{2,1,0:T(8,128)} %copy-done.1), custom_call_target="tpu_custom_call" | custom-call | tf_op jit(solution)/shard_map/remap/pallas_call | solution.py:131
  32.6 21.7 %all_to_all.10 = f32[32,72,128]{2,1,0:T(8,128)} all-to-all(f32[32,72,128]{2,1,0:T(8,128)} %remap.1), channel_id=1, replica_groups=mesh['az'=32,'rad'=8] {'az'}, dimensions={0} | all-to-all | bytes 2359296 | tf_op jit(solution)/shard_map/all_to_all | solution.py:138
  54.2 0.0 copy-start
  54.2 2.1 %edges.1 = (f32[5,64,128]{2,1,0:T(8,128)}, f32[5,64,128]{2,1,0:T(8,128)}) custom-call(f32[8,4,72,128]{3,2,1,0:T(8,128)} %bitcast.6), custom_call_target="tpu_custom_call" | custom-call | tf_op jit(solution)/shard_map/edges/pallas_call | solution.py:142
  56.4 8.0 %collective-permute-start = (f32[5,64,128]{2,1,0:T(8,128)}, f32[5,64,128]{2,1,0:T(8,128)S(1)}, u32[]{:S(2)}, u32[]{:S(2)}) collective-permute-start(f32[5,64,128]{2,1,0:T(8,128)} %get-tuple-element.7), channel_id=1, source_target_pairs={{0,1},{1,2},{2,3},{3,4},{4,5},{5,6},{6,7},{8,9},{9,10},{10,11},{11... | collective-permute-start | bytes 491528 | tf_op jit(solution)/shard_map/ppermute | solution.py:145
  64.3 1.9 %collective-permute-start.1 = (f32[5,64,128]{2,1,0:T(8,128)}, f32[5,64,128]{2,1,0:T(8,128)S(1)}, u32[]{:S(2)}, u32[]{:S(2)}) collective-permute-start(f32[5,64,128]{2,1,0:T(8,128)} %get-tuple-element.8), channel_id=1, source_target_pairs={{1,0},{2,1},{3,2},{4,3},{5,4},{6,5},{7,6},{9,8},{10,9},{11,10},{12... | collective-permute-start | bytes 491528 | tf_op jit(solution)/shard_map/ppermute | solution.py:146
  66.3 0.1 pad_add_fusion.first_ref
  66.4 0.6 collective-permute-done.below_ref
  67.0 6.9 %collective-permute-done.1.above_ref = f32[5,64,128]{2,1,0:T(8,128)S(1)} collective-permute-done((f32[5,64,128]{2,1,0:T(8,128)}, f32[5,64,128]{2,1,0:T(8,128)S(1)}, u32[]{:S(2)}, u32[]{:S(2)}) %collective-permute-start.1) | collective-permute-done | bytes 163872 | tf_op jit(solution)/shard_map/ppermute | solution.py:146
  73.9 0.0 copy-done
  73.9 2.5 %update.1 = f32[8,4,64,128]{3,2,1,0:T(8,128)} custom-call(s32[2]{0:T(128)S(1)} %pad_add_fusion.first_ref, f32[8,4,72,128]{3,2,1,0:T(8,128)S(1)} %bitcast.7, f32[5,64,128]{2,1,0:T(8,128)S(1)} %collective-permute-done.below_ref, f32[5,64,128]{2,1,0:T(8,128)S(1)} %collective-permute-done.1.above_ref), custom_call_target="tpu_custom_call" | custom-call | tf_op jit(solution)/shard_map/update/pallas_call | solution.py:148
Async XLA Ops:
  0.0 9.4 %copy-start.2 = (s32[4]{0:T(128)S(1)}, s32[4]{0:T(128)}, u32[]{:S(2)}) copy-start(s32[4]{0:T(128)} %param.4) | copy-start | bytes 52
  0.0 12.6 %copy-start.3 = (f32[4]{0:T(128)S(1)}, f32[4]{0:T(128)}, u32[]{:S(2)}) copy-start(f32[4]{0:T(128)} %param.5) | copy-start | bytes 52
  0.0 26.1 %all-to-all-start = ((f32[32,64,128]{2,1,0:T(8,128)}), f32[32,64,128]{2,1,0:T(8,128)S(1)}, u32[]{:S(2)}, u32[]{:S(2)}) async-start(f32[32,64,128]{2,1,0:T(8,128)} %bitcast.8), calls=%async_computation | async-start | bytes 2097152 | tf_op jit(solution)/shard_map/all_to_all | solution.py:126
  26.1 1.0 %copy-start.1 = (f32[32,64,128]{2,1,0:T(8,128)}, f32[32,64,128]{2,1,0:T(8,128)S(1)}, u32[]{:S(2)}) copy-start(f32[32,64,128]{2,1,0:T(8,128)S(1)} %all-to-all-done.x_ref) | copy-start | bytes 3145732
  54.2 19.6 %copy-start = (f32[32,72,128]{2,1,0:T(8,128)S(1)}, f32[32,72,128]{2,1,0:T(8,128)}, u32[]{:S(2)}) copy-start(f32[32,72,128]{2,1,0:T(8,128)} %all_to_all.10) | copy-start | bytes 3538948
  56.4 10.6 %collective-permute-start = (f32[5,64,128]{2,1,0:T(8,128)}, f32[5,64,128]{2,1,0:T(8,128)S(1)}, u32[]{:S(2)}, u32[]{:S(2)}) collective-permute-start(f32[5,64,128]{2,1,0:T(8,128)} %get-tuple-element.7), channel_id=1, source_target_pairs={{0,1},{1,2},{2,3},{3,4},{4,5},{5,6},{6,7},{8,9},{9,10},{10,11},{11... | collective-permute-start | bytes 491528 | tf_op jit(solution)/shard_map/ppermute | solution.py:145
  64.3 9.5 %collective-permute-start.1 = (f32[5,64,128]{2,1,0:T(8,128)}, f32[5,64,128]{2,1,0:T(8,128)S(1)}, u32[]{:S(2)}, u32[]{:S(2)}) collective-permute-start(f32[5,64,128]{2,1,0:T(8,128)} %get-tuple-element.8), channel_id=1, source_target_pairs={{1,0},{2,1},{3,2},{4,3},{5,4},{6,5},{7,6},{9,8},{10,9},{11,10},{12... | collective-permute-start | bytes 491528 | tf_op jit(solution)/shard_map/ppermute | solution.py:146

commit v2 on v1

--- a/solution.py
+++ b/solution.py
@@ -8,13 +8,16 @@
 F32 = jnp.float32
 VMEM = pl.BlockSpec(memory_space=pltpu.VMEM)
 SMEM = pl.BlockSpec(memory_space=pltpu.SMEM)
+GRANT = pltpu.CompilerParams(vmem_limit_bytes=16 * 2**20)
 
 
-def remap_kernel(steps_ref, frac_ref, x_ref, o_ref):
+def remap_kernel(shifts_ref, fracs_ref, x_ref, o_ref):
     blocks, height, width = x_ref.shape
-    block_shift = steps_ref[0]
-    lane_shift = steps_ref[1]
-    frac = frac_ref[0]
+    mine = lax.rem(lax.axis_index("az"), shifts_ref.shape[0])
+    shift = shifts_ref[mine]
+    frac = fracs_ref[mine]
+    block_shift = lax.div(shift, width)
+    lane_shift = lax.rem(shift, width)
     lane = lax.broadcasted_iota(jnp.int32, (height, width), 1)
     own = lane + lane_shift < width
     own_next = lane + lane_shift + 1 < width
@@ -50,19 +53,23 @@
     )
 
 
-def edge_kernel(s_ref, low_ref, high_ref):
+def edge_kernel(s_ref, chip_ref, far_ref):
     radii = s_ref.shape[1]
-    height = low_ref.shape[1]
-    for r, out in ((0, low_ref), (radii - 1, high_ref)):
+    height = chip_ref.shape[1]
+    odd = lax.rem(lax.axis_index("rad"), 2)
+    for r, out in ((jnp.where(odd == 1, 0, radii - 1), chip_ref), (jnp.where(odd == 1, radii - 1, 0), far_ref)):
         wx, wy, wz, fx, fy, fz, es, pm = products([s_ref[v, r, :height] for v in range(8)])
         for at, field in enumerate((wy, wz, fx, es, pm)):
             out[at] = field
 
 
-def update_kernel(first_ref, s_ref, below_ref, above_ref, o_ref, f_ref):
+def update_kernel(s_ref, chip_ref, far_ref, o_ref, f_ref):
     radii = s_ref.shape[1]
     height, width = o_ref.shape[2:]
-    total_radii = first_ref[1]
+    bands = lax.axis_size("rad")
+    band = lax.axis_index("rad")
+    odd = lax.rem(band, 2) == 1
+    total_radii = radii * bands
     pad = 8
     lane = lax.broadcasted_iota(jnp.int32, (height, width), 1)
     level = lax.broadcasted_iota(jnp.int32, (height, width), 0)
@@ -83,15 +90,21 @@
         jnp.concatenate([rows, jnp.zeros((width - used, width), F32)], axis=0)
     )[:height]
     spot = {0: 0, 2: 1, 4: 2, 6: 3, 7: 4}
+    place = {1: 0, 2: 1, 3: 2, 6: 3, 7: 4}
 
     for r in range(radii):
         rho, vx, vy, vz, bx, by, bz, ent = [s_ref[v, r, :height] for v in range(8)]
-        xr = ((first_ref[0] + r).astype(F32) + 0.5) / total_radii.astype(F32) - 0.5
-        place = {1: 0, 2: 1, 3: 2, 6: 3, 7: 4}
+        xr = ((band * radii + r).astype(F32) + 0.5) / total_radii - 0.5
 
         def dx(at):
-            plus = above_ref[place[at]] if r == radii - 1 else f_ref[at, r + 1, pad : pad + height]
-            minus = below_ref[place[at]] if r == 0 else f_ref[at, r - 1, pad : pad + height]
+            if r == radii - 1:
+                plus = jnp.where(odd, far_ref[place[at]], chip_ref[place[at]])
+            else:
+                plus = f_ref[at, r + 1, pad : pad + height]
+            if r == 0:
+                minus = jnp.where(odd, chip_ref[place[at]], far_ref[place[at]])
+            else:
+                minus = f_ref[at, r - 1, pad : pad + height]
             return 0.5 * (plus - minus)
 
         def dy(at):
@@ -122,38 +135,36 @@
     variables, radii, height, width = state.shape
     count = variables * radii
     bands = lax.axis_size("rad")
-    band = lax.axis_index("rad")
     turned = lax.all_to_all(state.reshape(count, height, width), "az", 0, 0, tiled=True)
-    mine = lax.axis_index("az") % radii
-    shift = lax.dynamic_index_in_dim(shifts, mine, keepdims=False)
-    frac = lax.dynamic_slice_in_dim(fracs, mine, 1)
-    steps = jnp.stack([shift // width, shift % width])
     moved = pl.pallas_call(
         remap_kernel,
         out_shape=jax.ShapeDtypeStruct((count, height + 8, width), F32),
         in_specs=[SMEM, SMEM, VMEM],
         out_specs=VMEM,
+        compiler_params=GRANT,
         name="remap",
-    )(steps, frac, turned)
+    )(shifts, fracs, turned)
     remapped = lax.all_to_all(moved, "az", 0, 0, tiled=True).reshape(
         variables, radii, height + 8, width
     )
     edge = jax.ShapeDtypeStruct((5, height, width), F32)
-    low, high = pl.pallas_call(
-        edge_kernel, out_shape=(edge, edge), in_specs=[VMEM], out_specs=(VMEM, VMEM), name="edges"
+    chip, far = pl.pallas_call(
+        edge_kernel, out_shape=(edge, edge), in_specs=[VMEM], out_specs=(VMEM, VMEM), name="edges",
+        compiler_params=GRANT,
     )(remapped)
-    below = lax.ppermute(high, "rad", [(i, i + 1) for i in range(bands - 1)])
-    above = lax.ppermute(low, "rad", [(i + 1, i) for i in range(bands - 1)])
-    places = jnp.stack([band * radii, bands * radii]).astype(jnp.int32)
+    inner = [(i, i ^ 1) for i in range(bands)]
+    outer = [(i, i + 1) for i in range(1, bands - 1, 2)] + [(i + 1, i) for i in range(1, bands - 1, 2)]
+    far = lax.ppermute(far, "rad", outer)
+    chip = lax.ppermute(chip, "rad", inner)
     return pl.pallas_call(
         update_kernel,
         out_shape=jax.ShapeDtypeStruct(state.shape, F32),
-        in_specs=[SMEM, VMEM, VMEM, VMEM],
+        in_specs=[VMEM, VMEM, VMEM],
         out_specs=VMEM,
         scratch_shapes=[pltpu.VMEM((8, radii, height + 16, width), F32)],
-        compiler_params=pltpu.CompilerParams(vmem_limit_bytes=32 * 2**20),
+        compiler_params=GRANT,
         name="update",
-    )(places, remapped, below, above)
+    )(remapped, chip, far)
 
 
 def solution(mesh):

time: 77.3 us -> 64.8 us (0.84)
  blocking collectives: 21.7 us -> 46.6 us
  waiting for transfers between devices: 19.7 us -> 4.74 us
  starting transfers between devices: 19.2 us -> 8.09 us
  Pallas kernels: 10.1 us -> 5.03 us
  between operations: 2.67 us -> 0.03 us
  local copies, waits for them, and re-layouts: 2.22 us -> 0.01 us
    all_to_all x0 -> x1, blocking collectives: none -> 26.1 us  [on_device(): lax.all_to_all(state.reshape(count, height, width), 'az', 0, 0, tiled=True)]
    all_to_all x1 -> x0, waiting for transfers between devices: 12.2 us -> none  [on_device(): lax.all_to_all(state.reshape(count, height, width), 'az', 0, 0, tiled=True)]
    all_to_all x1 -> x0, starting transfers between devices: 9.35 us -> none  [on_device(): lax.all_to_all(state.reshape(count, height, width), 'az', 0, 0, tiled=True)]
    ppermute x2, waiting for transfers between devices: 7.49 us -> 4.74 us  [the longest x1 4.73 us: on_device(): far = lax.ppermute(far, 'rad', outer)]
    pallas_call x1, Pallas kernels: 5.51 us -> 3.04 us  [on_device(): pl.pallas_call(remap_kernel, out_shape=jax.ShapeDtypeStruct((count, heigh...]
    pallas_call x1, Pallas kernels: 2.12 us -> 0.04 us  [on_device(): pl.pallas_call(edge_kernel, out_shape=(edge, edge), in_specs=[VMEM], out_...]
    ppermute x2, starting transfers between devices: 9.9 us -> 8.09 us  [the longest x1 4.8 us: on_device(): far = lax.ppermute(far, 'rad', outer)]
    dynamic_slice x2 -> x0, local copies, waits for them, and re-layouts: 1.24 us -> none  [the longest x1 0.66 us: on_device(): frac = lax.dynamic_slice_in_dim(fracs, mine, 1)]
  transfers between devices with their start and end apart: 3 -> 2, of which waited for: 3 -> 1; matrix products, arithmetic and copies ran while one was open for 3% -> 0% of each run, Pallas kernels for 0% -> 0%
where the time goes in v2:
time: 64.8 us; the launch traced here: 64.5 us
  blocking collectives  46.6 us (72%)
  starting transfers between devices  8.09 us (12%)
  Pallas kernels  5.03 us (8%)
  waiting for transfers between devices  4.74 us (7%)
    all_to_all x1, blocking collectives, on_device(): lax.all_to_all(state.reshape(count, height, width), 'az', 0, 0, tiled=True)  26.1 us
    all_to_all x1, blocking collectives, on_device(): lax.all_to_all(moved, 'az', 0, 0, tiled=True)  20.5 us
    ppermute x1, starting transfers between devices, on_device(): far = lax.ppermute(far, 'rad', outer)  4.8 us
    ppermute x1, waiting for transfers between devices, on_device(): far = lax.ppermute(far, 'rad', outer)  4.73 us
    ppermute x1, starting transfers between devices, on_device(): chip = lax.ppermute(chip, 'rad', inner)  3.29 us
    pallas_call x1, Pallas kernels, on_device(): pl.pallas_call(remap_kernel, out_shape=jax.ShapeDtypeStruct((count, heigh...  3.04 us
    pallas_call x1, Pallas kernels, on_device(): pl.pallas_call(update_kernel, out_shape=jax.ShapeDtypeStruct(state.shape,...  1.95 us
  transfers between devices with their start and end apart: 2, of which 1 were waited for; matrix products, arithmetic and copies ran while one was open for 0% of the time, Pallas kernels for 0%

profile of v2, /device:TPU:1, one launch (start us, length us, event | category | flops | bytes accessed | tf_op | source)
XLA Modules:
  0.0 64.5 jit_solution(5672525792332632883)
XLA Ops:
  0.0 0.0 copy-start.1
  0.0 0.0 copy-start
  0.0 26.1 %all_to_all.10.x_ref = f32[32,64,128]{2,1,0:T(8,128)S(1)} all-to-all(f32[32,64,128]{2,1,0:T(8,128)} %bitcast.4), channel_id=1, replica_groups=mesh['az'=32,'rad'=8] {'az'}, dimensions={0} | all-to-all | bytes 2097152 | tf_op jit(solution)/shard_map/all_to_all | solution.py:138
  26.1 0.0 copy-done.1
  26.1 0.0 copy-done
  26.1 3.0 %remap.1 = f32[32,72,128]{2,1,0:T(8,128)S(1)} custom-call(s32[4]{0:T(128)S(1)} %copy-done, f32[4]{0:T(128)S(1)} %copy-done.1, f32[32,64,128]{2,1,0:T(8,128)S(1)} %all_to_all.10.x_ref), custom_call_target="tpu_custom_call" | custom-call | tf_op jit(solution)/shard_map/remap/pallas_call | solution.py:139
  29.1 20.5 %all_to_all.11 = f32[32,72,128]{2,1,0:T(8,128)S(1)} all-to-all(f32[32,72,128]{2,1,0:T(8,128)S(1)} %remap.1), channel_id=1, replica_groups=mesh['az'=32,'rad'=8] {'az'}, dimensions={0} | all-to-all | bytes 2359296 | tf_op jit(solution)/shard_map/all_to_all | solution.py:147
  49.7 3.3 %collective-permute-start = (f32[5,64,128]{2,1,0:T(8,128)S(1)}, f32[5,64,128]{2,1,0:T(8,128)S(1)}, u32[]{:S(2)}, u32[]{:S(2)}) collective-permute-start(f32[5,64,128]{2,1,0:T(8,128)S(1)} %get-tuple-element.7), channel_id=1, source_target_pairs={{0,1},{1,0},{2,3},{3,2},{4,5},{5,4},{6,7},{7,6},{8,9},{9,8},{10,11... | collective-permute-start | bytes 491528 | tf_op jit(solution)/shard_map/ppermute | solution.py:158
  53.0 4.8 %collective-permute-start.1 = (f32[5,64,128]{2,1,0:T(8,128)S(1)}, f32[5,64,128]{2,1,0:T(8,128)S(1)}, u32[]{:S(2)}, u32[]{:S(2)}) collective-permute-start(f32[5,64,128]{2,1,0:T(8,128)S(1)} %get-tuple-element.8), channel_id=1, source_target_pairs={{1,2},{3,4},{5,6},{2,1},{4,3},{6,5},{9,10},{11,12},{13,14},{10,9},... | collective-permute-start | bytes 491528 | tf_op jit(solution)/shard_map/ppermute | solution.py:157
  57.8 0.0 collective-permute-done.chip_ref
  57.8 4.7 %collective-permute-done.1.far_ref = f32[5,64,128]{2,1,0:T(8,128)S(1)} collective-permute-done((f32[5,64,128]{2,1,0:T(8,128)S(1)}, f32[5,64,128]{2,1,0:T(8,128)S(1)}, u32[]{:S(2)}, u32[]{:S(2)}) %collective-permute-start.1) | collective-permute-done | bytes 163872 | tf_op jit(solution)/shard_map/ppermute | solution.py:157
  62.5 1.9 %update.1 = f32[8,4,64,128]{3,2,1,0:T(8,128)} custom-call(f32[8,4,72,128]{3,2,1,0:T(8,128)S(1)} %bitcast.3, f32[5,64,128]{2,1,0:T(8,128)S(1)} %collective-permute-done.chip_ref, f32[5,64,128]{2,1,0:T(8,128)S(1)} %collective-permute-done.1.far_ref), custom_call_target="tpu_custom_call" | custom-call | tf_op jit(solution)/shard_map/update/pallas_call | solution.py:159
  (1 shorter events, 0.0 us)
Async XLA Ops:
  0.0 26.1 %copy-start.1 = (f32[4]{0:T(128)S(1)}, f32[4]{0:T(128)}, u32[]{:S(2)}) copy-start(f32[4]{0:T(128)} %fracs_ref.1) | copy-start | bytes 52
  0.0 26.1 %copy-start = (s32[4]{0:T(128)S(1)}, s32[4]{0:T(128)}, u32[]{:S(2)}) copy-start(s32[4]{0:T(128)} %shifts_ref.1) | copy-start | bytes 52
  49.7 8.1 %collective-permute-start = (f32[5,64,128]{2,1,0:T(8,128)S(1)}, f32[5,64,128]{2,1,0:T(8,128)S(1)}, u32[]{:S(2)}, u32[]{:S(2)}) collective-permute-start(f32[5,64,128]{2,1,0:T(8,128)S(1)} %get-tuple-element.7), channel_id=1, source_target_pairs={{0,1},{1,0},{2,3},{3,2},{4,5},{5,4},{6,7},{7,6},{8,9},{9,8},{10,11... | collective-permute-start | bytes 491528 | tf_op jit(solution)/shard_map/ppermute | solution.py:158
  53.0 9.5 %collective-permute-start.1 = (f32[5,64,128]{2,1,0:T(8,128)S(1)}, f32[5,64,128]{2,1,0:T(8,128)S(1)}, u32[]{:S(2)}, u32[]{:S(2)}) collective-permute-start(f32[5,64,128]{2,1,0:T(8,128)S(1)} %get-tuple-element.8), channel_id=1, source_target_pairs={{1,2},{3,4},{5,6},{2,1},{4,3},{6,5},{9,10},{11,12},{13,14},{10,9},... | collective-permute-start | bytes 491528 | tf_op jit(solution)/shard_map/ppermute | solution.py:157

commit v3 on v2

v3 whole, which is shorter than its diff:
```python
import functools

import jax
import jax.numpy as jnp
from jax import lax
from jax.experimental import pallas as pl
from jax.experimental.pallas import tpu as pltpu
from jax.sharding import PartitionSpec as P

F32 = jnp.float32
VMEM = pl.BlockSpec(memory_space=pltpu.VMEM)
SMEM = pl.BlockSpec(memory_space=pltpu.SMEM)
ANY = pl.BlockSpec(memory_space=pl.ANY)
GRANT = pltpu.CompilerParams(vmem_limit_bytes=16 * 2**20)
ROWS = 8
EDGE_FIELDS = (1, 2, 3, 6, 7)
SIDE_FIELDS = (0, 2, 4, 6, 7)
EDGE_CHANGED = (0, 1, 5, 6, 7)
EDGE_SETTLED = (2, 3, 4)


def remap_kernel(shifts_ref, fracs_ref, x_ref, o_ref, ends_ref):
    blocks, height, width = x_ref.shape
    mine = lax.rem(lax.axis_index("az"), shifts_ref.shape[0])
    shift = shifts_ref[mine]
    frac = fracs_ref[mine]
    block_shift = lax.div(shift, width)
    lane_shift = lax.rem(shift, width)
    lane = lax.broadcasted_iota(jnp.int32, (height, width), 1)
    own = lane + lane_shift < width
    own_next = lane + lane_shift + 1 < width
    for i in range(blocks):
        near = x_ref[lax.rem(i - block_shift + blocks, blocks)]
        far = x_ref[lax.rem(i - block_shift - 1 + 2 * blocks, blocks)]
        first = pltpu.roll(jnp.where(own, near, far), lane_shift, 1)
        second = pltpu.roll(jnp.where(own_next, near, far), lane_shift + 1, 1)
        o_ref[i, :height, :] = (1.0 - frac) * first + frac * second
    slot = lax.broadcasted_iota(jnp.int32, (ROWS, width), 1)
    pair = lax.shift_right_logical(slot, 1)
    kept = [pair == k for k in range(height // ROWS)]
    for i in range(blocks):
        ends = jnp.zeros((ROWS, width), F32)
        for k in range(height // ROWS):
            turned = pltpu.roll(o_ref[i, k * ROWS : (k + 1) * ROWS, :], 2 * k + 1, 1)
            ends = jnp.where(kept[k], turned, ends)
        ends_ref[i] = ends
    odd = (slot & 1) == 1
    for i in range(blocks):
        before = pltpu.roll(ends_ref[(i - 1) % blocks], 1, 1)
        after = pltpu.roll(ends_ref[(i + 1) % blocks], width - 1, 1)
        o_ref[i, height:, :] = jnp.where(odd, before, after)


def products(S):
    rho, vx, vy, vz, bx, by, bz, ent = S
    return (
        vy * bz - vz * by,
        vz * bx - vx * bz,
        vx * by - vy * bx,
        rho * vx,
        rho * vy,
        rho * vz,
        ent,
        0.5 * (bx * bx + by * by + bz * bz),
    )


def edge_kernel(outward, s_ref, far_ref):
    height = far_ref.shape[1]
    odd = lax.rem(lax.axis_index("rad"), 2)
    r = (odd if outward else 1 - odd) * (s_ref.shape[1] - 1)
    fields = products([s_ref[v, r, :height] for v in range(8)])
    for at, field in enumerate(EDGE_FIELDS):
        far_ref[at] = fields[field]


def main_kernel(s_ref, o_ref, part_ref, f_ref, done_ref, sems):
    variables, radii, height, width = done_ref.shape
    bands = lax.axis_size("rad")
    band = lax.axis_index("rad")
    total_radii = radii * bands
    pad = ROWS
    lane = lax.broadcasted_iota(jnp.int32, (height, width), 1)
    level = lax.broadcasted_iota(jnp.int32, (height, width), 0)
    zk = (level.astype(F32) + 0.5) / height - 0.5
    for r in range(radii):
        for at, field in enumerate(products([s_ref[v, r, :height] for v in range(8)])):
            f_ref[at, r, pad : pad + height] = field
            f_ref[at, r, :pad] = jnp.zeros((pad, width), F32)
            f_ref[at, r, pad + height :] = jnp.zeros((pad, width), F32)
    copies = []
    for r in (1, 2, 0, 3):
        rho, vx, vy, vz, bx, by, bz, ent = [s_ref[v, r, :height] for v in range(8)]
        tails = products([s_ref[v, r, height:] for v in range(8)])
        xr = ((band * radii + r).astype(F32) + 0.5) / total_radii - 0.5
        outer = r == 0 or r == radii - 1

        def dx(at):
            if r == 0:
                return 0.5 * f_ref[at, 1, pad : pad + height]
            minus = f_ref[at, r - 1, pad : pad + height]
            if r == radii - 1:
                return -0.5 * minus
            return 0.5 * (f_ref[at, r + 1, pad : pad + height] - minus)

        def dy(at):
            here = f_ref[at, r, pad : pad + height]
            beside = jnp.concatenate(
                [pltpu.roll(tails[at], width - 2 * k - 1, 1) for k in range(height // ROWS)], axis=0
            )
            plus = jnp.where(lane == width - 1, beside, pltpu.roll(here, width - 1, 1))
            minus = jnp.where(lane == 0, beside, pltpu.roll(here, 1, 1))
            return 0.5 * (plus - minus)

        def dz(at):
            plus = f_ref[at, r, pad + 1 : pad + 1 + height]
            minus = f_ref[at, r, pad - 1 : pad - 1 + height]
            return 0.5 * (plus - minus)

        new = (
            rho + 0.2 * -(dx(3) + dy(4) + dz(5)),
            vx + 0.2 * (2.0 * vy + 3.0 * xr - dx(7)),
            vy + 0.2 * (-0.5 * vx - dy(7)),
            vz + 0.2 * (-zk - dz(7)),
            bx + 0.2 * (dy(2) - dz(1)),
            by + 0.2 * (dz(0) - dx(2)),
            bz + 0.2 * (dx(1) - dy(0)),
            ent + 0.2 * -(vx * dx(6) + vy * dy(6) + vz * dz(6)),
        )
        for v in range(variables):
            if outer and v in EDGE_CHANGED:
                part_ref[EDGE_CHANGED.index(v), r // (radii - 1)] = new[v]
            else:
                done_ref[v, r] = new[v]
        span = slice(EDGE_SETTLED[0], EDGE_SETTLED[-1] + 1) if outer else slice(0, variables)
        copy = pltpu.make_async_copy(done_ref.at[span, r], o_ref.at[span, r], sems.at[r])
        copy.start()
        copies.append(copy)
    for copy in copies:
        copy.wait()


def finish_kernel(base_ref, s_ref, part_ref, far_ref, chip_ref, o_ref, done_ref, sems):
    del base_ref
    radii = s_ref.shape[1]
    height = chip_ref.shape[1]
    odd = lax.rem(lax.axis_index("rad"), 2) == 1
    copies = []
    for pair in range(2):
        r = pair * (radii - 1)
        step = 0.1 if pair else -0.1
        halo = []
        for at in range(len(EDGE_FIELDS)):
            up, down = (far_ref, chip_ref) if pair else (chip_ref, far_ref)
            halo.append(step * jnp.where(odd, up[at], down[at]))
        wy, wz, fx, es, pm = halo
        vx = s_ref[1, r, :height]
        changes = (-fx, -pm, -wz, wy, -(vx * es))
        for at, v in enumerate(EDGE_CHANGED):
            done_ref[at, pair] = part_ref[at, pair] + changes[at]
            copy = pltpu.make_async_copy(done_ref.at[at, pair], o_ref.at[v, r], sems.at[at, pair])
            copy.start()
            copies.append(copy)
    for copy in copies:
        copy.wait()


def on_device(state, shifts, fracs):
    variables, radii, height, width = state.shape
    count = variables * radii
    bands = lax.axis_size("rad")
    turned = lax.all_to_all(state.reshape(count, height, width), "az", 0, 0, tiled=True)
    moved = pl.pallas_call(
        remap_kernel,
        out_shape=jax.ShapeDtypeStruct((count, height + ROWS, width), F32),
        in_specs=[SMEM, SMEM, VMEM],
        out_specs=VMEM,
        scratch_shapes=[pltpu.VMEM((count, ROWS, width), F32)],
        compiler_params=GRANT,
        name="remap",
    )(shifts, fracs, turned)
    remapped = lax.all_to_all(moved, "az", 0, 0, tiled=True).reshape(
        variables, radii, height + ROWS, width
    )
    edge = jax.ShapeDtypeStruct((len(EDGE_FIELDS), height, width), F32)
    far, chip = [
        pl.pallas_call(
            functools.partial(edge_kernel, outward),
            out_shape=edge,
            in_specs=[VMEM],
            out_specs=VMEM,
            compiler_params=GRANT,
            name="far_edge" if outward else "chip_edge",
        )(remapped)
        for outward in (True, False)
    ]
    odd = range(1, bands - 1, 2)
    far = lax.ppermute(far, "rad", [(i, i + 1) for i in odd] + [(i + 1, i) for i in odd])
    chip = lax.ppermute(chip, "rad", [(i, i ^ 1) for i in range(bands)])
    changed = len(EDGE_CHANGED)
    whole = jax.ShapeDtypeStruct(state.shape, F32)
    settled, part = pl.pallas_call(
        main_kernel,
        out_shape=(whole, jax.ShapeDtypeStruct((changed, 2, height, width), F32)),
        in_specs=[VMEM],
        out_specs=(ANY, VMEM),
        scratch_shapes=[
            pltpu.VMEM((8, radii, height + 2 * ROWS, width), F32),
            pltpu.VMEM(state.shape, F32),
            pltpu.SemaphoreType.DMA((radii,)),
        ],
        compiler_params=GRANT,
        cost_estimate=pl.CostEstimate(flops=4 * 10**6, bytes_accessed=4 * 2**20, transcendentals=0),
        name="main",
    )(remapped)
    return pl.pallas_call(
        finish_kernel,
        out_shape=whole,
        in_specs=[ANY, VMEM, VMEM, VMEM, VMEM],
        out_specs=ANY,
        scratch_shapes=[
            pltpu.VMEM((changed, 2, height, width), F32),
            pltpu.SemaphoreType.DMA((changed, 2)),
        ],
        input_output_aliases={0: 0},
        compiler_params=GRANT,
        name="finish",
    )(settled, remapped, part, far, chip)


def solution(mesh):
    in_specs = (P(None, "rad", None, "az"), P("rad"), P("rad"))
    out_specs = P(None, "rad", None, "az")
    return jax.shard_map(
        on_device, mesh=mesh, in_specs=in_specs, out_specs=out_specs, check_vma=False
    )
```

time: 64.8 us -> 62 us (0.957)
  Pallas kernels: 5.03 us -> 3.67 us
  waiting for transfers between devices: 4.74 us -> 3.4 us
    pallas_call x1, Pallas kernels: 3.04 us -> 1.57 us  [on_device(): pl.pallas_call(remap_kernel, out_shape=jax.ShapeDtypeStruct((count, heigh...]
    ppermute x2, waiting for transfers between devices: 4.74 us -> 3.4 us  [the longest x1 3.4 us: on_device(): lax.ppermute(far, 'rad', [(i, i + 1) for i in odd] + [(i + 1, i) for i in...]
    pallas_call x2 -> x4, Pallas kernels: 1.98 us -> 2.1 us  [the longest x1 1.23 us: on_device(): pl.pallas_call(main_kernel, out_shape=(whole, jax.ShapeDtypeStruct((chang...]
  transfers between devices with their start and end apart: 2 -> 2, of which waited for: 1 -> 1; matrix products, arithmetic and copies ran while one was open for 0% -> 0% of each run, Pallas kernels for 0% -> 2%
where the time goes in v3:
time: 62 us; the launch traced here: 61.8 us
  blocking collectives  46.6 us (75%)
  starting transfers between devices  8.08 us (13%)
  Pallas kernels  3.67 us (6%)
  waiting for transfers between devices  3.4 us (5%)
    all_to_all x1, blocking collectives, on_device(): lax.all_to_all(state.reshape(count, height, width), 'az', 0, 0, tiled=True)  26.1 us
    all_to_all x1, blocking collectives, on_device(): lax.all_to_all(moved, 'az', 0, 0, tiled=True)  20.5 us
    ppermute x1, starting transfers between devices, on_device(): lax.ppermute(far, 'rad', [(i, i + 1) for i in odd] + [(i + 1, i) for i in...  7.99 us
    ppermute x1, waiting for transfers between devices, on_device(): lax.ppermute(far, 'rad', [(i, i + 1) for i in odd] + [(i + 1, i) for i in...  3.4 us
    pallas_call x1, Pallas kernels, on_device(): pl.pallas_call(remap_kernel, out_shape=jax.ShapeDtypeStruct((count, heigh...  1.57 us
  transfers between devices with their start and end apart: 2, of which 1 were waited for; matrix products, arithmetic and copies ran while one was open for 0% of the time, Pallas kernels for 2%

profile of v3, /device:TPU:1, one launch (start us, length us, event | category | flops | bytes accessed | tf_op | source)
XLA Modules:
  0.0 61.8 jit_solution(7661136023950049567)
XLA Ops:
  0.0 0.0 copy-start.1
  0.0 0.0 copy-start
  0.0 26.1 %all_to_all.10.x_ref = f32[32,64,128]{2,1,0:T(8,128)S(1)} all-to-all(f32[32,64,128]{2,1,0:T(8,128)} %bitcast.6), channel_id=1, replica_groups=mesh['az'=32,'rad'=8] {'az'}, dimensions={0} | all-to-all | bytes 2097152 | tf_op jit(solution)/shard_map/all_to_all | solution.py:172
  26.1 0.0 copy-done.1
  26.1 0.0 copy-done
  26.1 1.6 %remap.1 = f32[32,72,128]{2,1,0:T(8,128)S(1)} custom-call(s32[4]{0:T(128)S(1)} %copy-done, f32[4]{0:T(128)S(1)} %copy-done.1, f32[32,64,128]{2,1,0:T(8,128)S(1)} %all_to_all.10.x_ref), custom_call_target="tpu_custom_call" | custom-call | tf_op jit(solution)/shard_map/remap/pallas_call | solution.py:173
  27.7 20.5 %all_to_all.11 = f32[32,72,128]{2,1,0:T(8,128)S(1)} all-to-all(f32[32,72,128]{2,1,0:T(8,128)S(1)} %remap.1), channel_id=1, replica_groups=mesh['az'=32,'rad'=8] {'az'}, dimensions={0} | all-to-all | bytes 2359296 | tf_op jit(solution)/shard_map/all_to_all | solution.py:182
  48.2 8.0 %collective-permute-start = (f32[5,64,128]{2,1,0:T(8,128)S(1)}, f32[5,64,128]{2,1,0:T(8,128)S(1)}, u32[]{:S(2)}, u32[]{:S(2)}) collective-permute-start(f32[5,64,128]{2,1,0:T(8,128)S(1)} %far_edge.1), channel_id=1, source_target_pairs={{1,2},{3,4},{5,6},{2,1},{4,3},{6,5},{9,10},{11,12},{13,14},{10,9},... | collective-permute-start | bytes 491528 | tf_op jit(solution)/shard_map/ppermute | solution.py:198
  56.2 0.1 collective-permute-start.1
  56.3 1.2 %main.1 = (f32[8,4,64,128]{3,2,1,0:T(8,128)}, f32[5,2,64,128]{3,2,1,0:T(8,128)S(1)}) custom-call(f32[8,4,72,128]{3,2,1,0:T(8,128)S(1)} %bitcast.4), custom_call_target="tpu_custom_call" | custom-call | flops 4000000 | bytes 4194304 | tf_op jit(solution)/shard_map/main/pallas_call | solution.py:202
  57.6 3.4 %collective-permute-done.far_ref = f32[5,64,128]{2,1,0:T(8,128)S(1)} collective-permute-done((f32[5,64,128]{2,1,0:T(8,128)S(1)}, f32[5,64,128]{2,1,0:T(8,128)S(1)}, u32[]{:S(2)}, u32[]{:S(2)}) %collective-permute-start) | collective-permute-done | bytes 163872 | tf_op jit(solution)/shard_map/ppermute | solution.py:198
  61.0 0.0 collective-permute-done.1.chip_ref
  61.0 0.8 %finish.1 = f32[8,4,64,128]{3,2,1,0:T(8,128)} custom-call(f32[8,4,64,128]{3,2,1,0:T(8,128)} %get-tuple-element.7.base_ref, f32[8,4,72,128]{3,2,1,0:T(8,128)S(1)} %bitcast.5, f32[5,2,64,128]{3,2,1,0:T(8,128)S(1)} %get-tuple-element.8.part_ref, f32[5,64,128]{2,1,0:T(8,128)S(1)} %collective-permute-done.far_ref, ...), custom_call_target="tpu_custom_call", output_to_operand_aliasing={{}: (0, {})} | custom-call | tf_op jit(solution)/shard_map/finish/pallas_call | solution.py:216
  (2 shorter events, 0.1 us)
Async XLA Ops:
  0.0 26.1 %copy-start.1 = (f32[4]{0:T(128)S(1)}, f32[4]{0:T(128)}, u32[]{:S(2)}) copy-start(f32[4]{0:T(128)} %fracs_ref.1) | copy-start | bytes 52
  0.0 26.1 %copy-start = (s32[4]{0:T(128)S(1)}, s32[4]{0:T(128)}, u32[]{:S(2)}) copy-start(s32[4]{0:T(128)} %shifts_ref.1) | copy-start | bytes 52
  48.2 12.7 %collective-permute-start = (f32[5,64,128]{2,1,0:T(8,128)S(1)}, f32[5,64,128]{2,1,0:T(8,128)S(1)}, u32[]{:S(2)}, u32[]{:S(2)}) collective-permute-start(f32[5,64,128]{2,1,0:T(8,128)S(1)} %far_edge.1), channel_id=1, source_target_pairs={{1,2},{3,4},{5,6},{2,1},{4,3},{6,5},{9,10},{11,12},{13,14},{10,9},... | collective-permute-start | bytes 491528 | tf_op jit(solution)/shard_map/ppermute | solution.py:198
  56.2 4.7 %collective-permute-start.1 = (f32[5,64,128]{2,1,0:T(8,128)S(1)}, f32[5,64,128]{2,1,0:T(8,128)S(1)}, u32[]{:S(2)}, u32[]{:S(2)}) collective-permute-start(f32[5,64,128]{2,1,0:T(8,128)S(1)} %chip_edge.1), channel_id=1, source_target_pairs={{0,1},{1,0},{2,3},{3,2},{4,5},{5,4},{6,7},{7,6},{8,9},{9,8},{10,11... | collective-permute-start | bytes 491528 | tf_op jit(solution)/shard_map/ppermute | solution.py:199

commit v4 on v3

--- a/solution.py
+++ b/solution.py
@@ -21,6 +21,7 @@
 
 def remap_kernel(shifts_ref, fracs_ref, x_ref, o_ref, ends_ref):
     blocks, height, width = x_ref.shape
+    tall = height + 1
     mine = lax.rem(lax.axis_index("az"), shifts_ref.shape[0])
     shift = shifts_ref[mine]
     frac = fracs_ref[mine]
@@ -34,21 +35,25 @@
         far = x_ref[lax.rem(i - block_shift - 1 + 2 * blocks, blocks)]
         first = pltpu.roll(jnp.where(own, near, far), lane_shift, 1)
         second = pltpu.roll(jnp.where(own_next, near, far), lane_shift + 1, 1)
-        o_ref[i, :height, :] = (1.0 - frac) * first + frac * second
-    slot = lax.broadcasted_iota(jnp.int32, (ROWS, width), 1)
-    pair = lax.shift_right_logical(slot, 1)
-    kept = [pair == k for k in range(height // ROWS)]
+        o_ref[tall * i : tall * i + height, :] = (1.0 - frac) * first + frac * second
+    pair = lax.shift_right_logical(lane, 1)
+    ends = jnp.zeros((height, width), F32)
     for i in range(blocks):
-        ends = jnp.zeros((ROWS, width), F32)
-        for k in range(height // ROWS):
-            turned = pltpu.roll(o_ref[i, k * ROWS : (k + 1) * ROWS, :], 2 * k + 1, 1)
-            ends = jnp.where(kept[k], turned, ends)
-        ends_ref[i] = ends
-    odd = (slot & 1) == 1
+        cells = o_ref[tall * i : tall * i + height, :]
+        ends = jnp.where(pair == i, pltpu.roll(cells, (2 * i + 1) % width, 1), ends)
+    rows = jnp.transpose(jnp.concatenate([ends, jnp.zeros((width - height, width), F32)], axis=0))
+    used = 2 * blocks
+    ends_ref[0] = rows[:used]
+    ends_ref[1] = pltpu.roll(rows[:used], height, 1)
     for i in range(blocks):
-        before = pltpu.roll(ends_ref[(i - 1) % blocks], 1, 1)
-        after = pltpu.roll(ends_ref[(i + 1) % blocks], width - 1, 1)
-        o_ref[i, height:, :] = jnp.where(odd, before, after)
+        last = 2 * ((i - 1) % blocks)
+        head = 2 * ((i + 1) % blocks) + 1
+        at = tall * i + height
+        o_ref[at : at + 1, :] = ends_ref[0, last : last + 1, :] + ends_ref[1, head : head + 1, :]
+
+
+def slab(s_ref, at, height):
+    return s_ref[at * (height + 1) : at * (height + 1) + height]
 
 
 def products(S):
@@ -65,13 +70,14 @@
     )
 
 
-def edge_kernel(outward, s_ref, far_ref):
+def edge_kernel(radii, s_ref, far_ref, chip_ref):
     height = far_ref.shape[1]
-    odd = lax.rem(lax.axis_index("rad"), 2)
-    r = (odd if outward else 1 - odd) * (s_ref.shape[1] - 1)
-    fields = products([s_ref[v, r, :height] for v in range(8)])
+    odd = lax.rem(lax.axis_index("rad"), 2) == 1
+    low = products([slab(s_ref, v * radii, height) for v in range(8)])
+    high = products([slab(s_ref, v * radii + radii - 1, height) for v in range(8)])
     for at, field in enumerate(EDGE_FIELDS):
-        far_ref[at] = fields[field]
+        far_ref[at] = jnp.where(odd, high[field], low[field])
+        chip_ref[at] = jnp.where(odd, low[field], high[field])
 
 
 def main_kernel(s_ref, o_ref, part_ref, f_ref, done_ref, sems):
@@ -80,18 +86,21 @@
     band = lax.axis_index("rad")
     total_radii = radii * bands
     pad = ROWS
+    tall = height + 1
+    side = lax.broadcasted_iota(jnp.int32, (ROWS, width), 1)
+    spot = lax.broadcasted_iota(jnp.int32, (ROWS, width), 0) + jnp.where(side == 0, 0, height)
     lane = lax.broadcasted_iota(jnp.int32, (height, width), 1)
     level = lax.broadcasted_iota(jnp.int32, (height, width), 0)
     zk = (level.astype(F32) + 0.5) / height - 0.5
     for r in range(radii):
-        for at, field in enumerate(products([s_ref[v, r, :height] for v in range(8)])):
+        for at, field in enumerate(products([slab(s_ref, v * radii + r, height) for v in range(8)])):
             f_ref[at, r, pad : pad + height] = field
             f_ref[at, r, :pad] = jnp.zeros((pad, width), F32)
             f_ref[at, r, pad + height :] = jnp.zeros((pad, width), F32)
     copies = []
     for r in (1, 2, 0, 3):
-        rho, vx, vy, vz, bx, by, bz, ent = [s_ref[v, r, :height] for v in range(8)]
-        tails = products([s_ref[v, r, height:] for v in range(8)])
+        rho, vx, vy, vz, bx, by, bz, ent = [slab(s_ref, v * radii + r, height) for v in range(8)]
+        tails = products([s_ref[(v * radii + r) * tall + height : (v * radii + r + 1) * tall] for v in range(8)])
         xr = ((band * radii + r).astype(F32) + 0.5) / total_radii - 0.5
         outer = r == 0 or r == radii - 1
 
@@ -105,11 +114,16 @@
 
         def dy(at):
             here = f_ref[at, r, pad : pad + height]
-            beside = jnp.concatenate(
-                [pltpu.roll(tails[at], width - 2 * k - 1, 1) for k in range(height // ROWS)], axis=0
+            row = jnp.broadcast_to(tails[at], (ROWS, width))
+            next_to = jnp.concatenate(
+                [
+                    jnp.take_along_axis(row, spot + k * ROWS, axis=1, mode="promise_in_bounds")
+                    for k in range(height // ROWS)
+                ],
+                axis=0,
             )
-            plus = jnp.where(lane == width - 1, beside, pltpu.roll(here, width - 1, 1))
-            minus = jnp.where(lane == 0, beside, pltpu.roll(here, 1, 1))
+            plus = jnp.where(lane == width - 1, next_to, pltpu.roll(here, width - 1, 1))
+            minus = jnp.where(lane == 0, next_to, pltpu.roll(here, 1, 1))
             return 0.5 * (plus - minus)
 
         def dz(at):
@@ -140,9 +154,8 @@
         copy.wait()
 
 
-def finish_kernel(base_ref, s_ref, part_ref, far_ref, chip_ref, o_ref, done_ref, sems):
+def finish_kernel(radii, base_ref, s_ref, part_ref, far_ref, chip_ref, o_ref, done_ref, sems):
     del base_ref
-    radii = s_ref.shape[1]
     height = chip_ref.shape[1]
     odd = lax.rem(lax.axis_index("rad"), 2) == 1
     copies = []
@@ -154,7 +167,7 @@
             up, down = (far_ref, chip_ref) if pair else (chip_ref, far_ref)
             halo.append(step * jnp.where(odd, up[at], down[at]))
         wy, wz, fx, es, pm = halo
-        vx = s_ref[1, r, :height]
+        vx = slab(s_ref, radii + r, height)
         changes = (-fx, -pm, -wz, wy, -(vx * es))
         for at, v in enumerate(EDGE_CHANGED):
             done_ref[at, pair] = part_ref[at, pair] + changes[at]
@@ -172,28 +185,24 @@
     turned = lax.all_to_all(state.reshape(count, height, width), "az", 0, 0, tiled=True)
     moved = pl.pallas_call(
         remap_kernel,
-        out_shape=jax.ShapeDtypeStruct((count, height + ROWS, width), F32),
+        out_shape=jax.ShapeDtypeStruct((count * (height + 1), width), F32),
         in_specs=[SMEM, SMEM, VMEM],
         out_specs=VMEM,
-        scratch_shapes=[pltpu.VMEM((count, ROWS, width), F32)],
+        scratch_shapes=[pltpu.VMEM((2, 2 * count, width), F32)],
         compiler_params=GRANT,
         name="remap",
     )(shifts, fracs, turned)
-    remapped = lax.all_to_all(moved, "az", 0, 0, tiled=True).reshape(
-        variables, radii, height + ROWS, width
-    )
+    moved = moved.reshape(count, height + 1, 1, width)
+    remapped = lax.all_to_all(moved, "az", 0, 0, tiled=True).reshape(count * (height + 1), width)
     edge = jax.ShapeDtypeStruct((len(EDGE_FIELDS), height, width), F32)
-    far, chip = [
-        pl.pallas_call(
-            functools.partial(edge_kernel, outward),
-            out_shape=edge,
-            in_specs=[VMEM],
-            out_specs=VMEM,
-            compiler_params=GRANT,
-            name="far_edge" if outward else "chip_edge",
-        )(remapped)
-        for outward in (True, False)
-    ]
+    far, chip = pl.pallas_call(
+        functools.partial(edge_kernel, radii),
+        out_shape=(edge, edge),
+        in_specs=[VMEM],
+        out_specs=(VMEM, VMEM),
+        compiler_params=GRANT,
+        name="edges",
+    )(remapped)
     odd = range(1, bands - 1, 2)
     far = lax.ppermute(far, "rad", [(i, i + 1) for i in odd] + [(i + 1, i) for i in odd])
     chip = lax.ppermute(chip, "rad", [(i, i ^ 1) for i in range(bands)])
@@ -214,7 +223,7 @@
         name="main",
     )(remapped)
     return pl.pallas_call(
-        finish_kernel,
+        functools.partial(finish_kernel, radii),
         out_shape=whole,
         in_specs=[ANY, VMEM, VMEM, VMEM, VMEM],
         out_specs=ANY,

time: 62 us -> 60.9 us (0.982)
  blocking collectives: 46.6 us -> 45.9 us
    all_to_all x1, blocking collectives: 20.5 us -> 19.9 us  [on_device(): lax.all_to_all(moved, 'az', 0, 0, tiled=True)]
    pallas_call x4 -> x3, Pallas kernels: 2.43 us -> 2.45 us  [the longest x1 1.59 us: on_device(): pl.pallas_call(remap_kernel, out_shape=jax.ShapeDtypeStruct((count * (hei...]
where the time goes in v4:
time: 60.9 us; the launch traced here: 60.7 us
  blocking collectives  45.9 us (75%)
  starting transfers between devices  7.64 us (13%)
  Pallas kernels  3.96 us (7%)
  waiting for transfers between devices  3.12 us (5%)
    all_to_all x1, blocking collectives, on_device(): lax.all_to_all(state.reshape(count, height, width), 'az', 0, 0, tiled=True)  26.1 us
    all_to_all x1, blocking collectives, on_device(): lax.all_to_all(moved, 'az', 0, 0, tiled=True)  19.9 us
    ppermute x1, starting transfers between devices, on_device(): lax.ppermute(far, 'rad', [(i, i + 1) for i in odd] + [(i + 1, i) for i in...  7.55 us
    ppermute x1, waiting for transfers between devices, on_device(): lax.ppermute(far, 'rad', [(i, i + 1) for i in odd] + [(i + 1, i) for i in...  3.12 us
    pallas_call x1, Pallas kernels, on_device(): pl.pallas_call(remap_kernel, out_shape=jax.ShapeDtypeStruct((count * (hei...  1.59 us
    pallas_call x1, Pallas kernels, on_device(): pl.pallas_call(main_kernel, out_shape=(whole, jax.ShapeDtypeStruct((chang...  1.51 us
  transfers between devices with their start and end apart: 2, of which 1 were waited for; matrix products, arithmetic and copies ran while one was open for 0% of the time, Pallas kernels for 2%

profile of v4, /device:TPU:1, one launch (start us, length us, event | category | flops | bytes accessed | tf_op | source)
XLA Modules:
  0.0 60.7 jit_solution(14738713851067798201)
XLA Ops:
  0.0 0.0 copy-start.1
  0.0 0.0 copy-start
  0.0 26.1 %all_to_all.10.x_ref = f32[32,64,128]{2,1,0:T(8,128)S(1)} all-to-all(f32[32,64,128]{2,1,0:T(8,128)} %bitcast.7), channel_id=1, replica_groups=mesh['az'=32,'rad'=8] {'az'}, dimensions={0} | all-to-all | bytes 2097152 | tf_op jit(solution)/shard_map/all_to_all | solution.py:185
  26.1 0.0 copy-done.1
  26.1 0.0 copy-done
  26.1 1.6 %remap.1 = f32[2080,128]{1,0:T(8,128)S(1)} custom-call(s32[4]{0:T(128)S(1)} %copy-done, f32[4]{0:T(128)S(1)} %copy-done.1, f32[32,64,128]{2,1,0:T(8,128)S(1)} %all_to_all.10.x_ref), custom_call_target="tpu_custom_call" | custom-call | tf_op jit(solution)/shard_map/remap/pallas_call | solution.py:186
  27.7 19.9 %all_to_all.11 = f32[32,65,1,128]{3,2,1,0:T(1,128)S(1)} all-to-all(f32[32,65,1,128]{3,2,1,0:T(1,128)S(1)} %bitcast.6), channel_id=1, replica_groups=mesh['az'=32,'rad'=8] {'az'}, dimensions={0} | all-to-all | bytes 2129920 | tf_op jit(solution)/shard_map/all_to_all | solution.py:196
  47.6 7.5 %collective-permute-start = (f32[5,64,128]{2,1,0:T(8,128)S(1)}, f32[5,64,128]{2,1,0:T(8,128)S(1)}, u32[]{:S(2)}, u32[]{:S(2)}) collective-permute-start(f32[5,64,128]{2,1,0:T(8,128)S(1)} %get-tuple-element.11), channel_id=1, source_target_pairs={{1,2},{3,4},{5,6},{2,1},{4,3},{6,5},{9,10},{11,12},{13,14},{10,9},... | collective-permute-start | bytes 491528 | tf_op jit(solution)/shard_map/ppermute | solution.py:207
  55.2 0.1 collective-permute-start.1
  55.3 1.5 %main.1 = (f32[8,4,64,128]{3,2,1,0:T(8,128)}, f32[5,2,64,128]{3,2,1,0:T(8,128)S(1)}) custom-call(f32[2080,128]{1,0:T(8,128)S(1)} %bitcast.4), custom_call_target="tpu_custom_call" | custom-call | flops 4000000 | bytes 4194304 | tf_op jit(solution)/shard_map/main/pallas_call | solution.py:211
  56.8 3.1 %collective-permute-done.far_ref = f32[5,64,128]{2,1,0:T(8,128)S(1)} collective-permute-done((f32[5,64,128]{2,1,0:T(8,128)S(1)}, f32[5,64,128]{2,1,0:T(8,128)S(1)}, u32[]{:S(2)}, u32[]{:S(2)}) %collective-permute-start) | collective-permute-done | bytes 163872 | tf_op jit(solution)/shard_map/ppermute | solution.py:207
  59.9 0.0 collective-permute-done.1.chip_ref
  59.9 0.8 %finish.1 = f32[8,4,64,128]{3,2,1,0:T(8,128)} custom-call(f32[8,4,64,128]{3,2,1,0:T(8,128)} %get-tuple-element.9.base_ref, f32[2080,128]{1,0:T(8,128)S(1)} %bitcast.5, f32[5,2,64,128]{3,2,1,0:T(8,128)S(1)} %get-tuple-element.10.part_ref, f32[5,64,128]{2,1,0:T(8,128)S(1)} %collective-permute-done.far_ref, ...), custom_call_target="tpu_custom_call", output_to_operand_aliasing={{}: (0, {})} | custom-call | tf_op jit(solution)/shard_map/finish/pallas_call | solution.py:225
  (1 shorter events, 0.0 us)
Async XLA Ops:
  0.0 26.1 %copy-start.1 = (f32[4]{0:T(128)S(1)}, f32[4]{0:T(128)}, u32[]{:S(2)}) copy-start(f32[4]{0:T(128)} %fracs_ref.1) | copy-start | bytes 52
  0.0 26.1 %copy-start = (s32[4]{0:T(128)S(1)}, s32[4]{0:T(128)}, u32[]{:S(2)}) copy-start(s32[4]{0:T(128)} %shifts_ref.1) | copy-start | bytes 52
  47.6 12.3 %collective-permute-start = (f32[5,64,128]{2,1,0:T(8,128)S(1)}, f32[5,64,128]{2,1,0:T(8,128)S(1)}, u32[]{:S(2)}, u32[]{:S(2)}) collective-permute-start(f32[5,64,128]{2,1,0:T(8,128)S(1)} %get-tuple-element.11), channel_id=1, source_target_pairs={{1,2},{3,4},{5,6},{2,1},{4,3},{6,5},{9,10},{11,12},{13,14},{10,9},... | collective-permute-start | bytes 491528 | tf_op jit(solution)/shard_map/ppermute | solution.py:207
  55.2 4.7 %collective-permute-start.1 = (f32[5,64,128]{2,1,0:T(8,128)S(1)}, f32[5,64,128]{2,1,0:T(8,128)S(1)}, u32[]{:S(2)}, u32[]{:S(2)}) collective-permute-start(f32[5,64,128]{2,1,0:T(8,128)S(1)} %get-tuple-element.12), channel_id=1, source_target_pairs={{0,1},{1,0},{2,3},{3,2},{4,5},{5,4},{6,7},{7,6},{8,9},{9,8},{10,11... | collective-permute-start | bytes 491528 | tf_op jit(solution)/shard_map/ppermute | solution.py:208

commit v5 on v4

--- a/solution.py
+++ b/solution.py
@@ -154,7 +154,12 @@
         copy.wait()
 
 
-def finish_kernel(radii, base_ref, s_ref, part_ref, far_ref, chip_ref, o_ref, done_ref, sems):
+def relay_kernel(from_ref, part_ref, to_ref):
+    del part_ref
+    to_ref[...] = from_ref[...]
+
+
+def finish_kernel(radii, base_ref, s_ref, part_ref, below_ref, chip_ref, above_ref, o_ref, done_ref, sems):
     del base_ref
     height = chip_ref.shape[1]
     odd = lax.rem(lax.axis_index("rad"), 2) == 1
@@ -164,8 +169,9 @@
         step = 0.1 if pair else -0.1
         halo = []
         for at in range(len(EDGE_FIELDS)):
-            up, down = (far_ref, chip_ref) if pair else (chip_ref, far_ref)
-            halo.append(step * jnp.where(odd, up[at], down[at]))
+            outside = above_ref[at] if pair else below_ref[at]
+            far_here = odd if pair else jnp.logical_not(odd)
+            halo.append(step * jnp.where(far_here, outside, chip_ref[at]))
         wy, wz, fx, es, pm = halo
         vx = slab(s_ref, radii + r, height)
         changes = (-fx, -pm, -wz, wy, -(vx * es))
@@ -204,7 +210,8 @@
         name="edges",
     )(remapped)
     odd = range(1, bands - 1, 2)
-    far = lax.ppermute(far, "rad", [(i, i + 1) for i in odd] + [(i + 1, i) for i in odd])
+    relayed = lax.ppermute(far, "rad", [(i, i + 2) for i in odd])
+    above = lax.ppermute(far, "rad", [(i + 1, i) for i in odd])
     chip = lax.ppermute(chip, "rad", [(i, i ^ 1) for i in range(bands)])
     changed = len(EDGE_CHANGED)
     whole = jax.ShapeDtypeStruct(state.shape, F32)
@@ -219,13 +226,22 @@
             pltpu.SemaphoreType.DMA((radii,)),
         ],
         compiler_params=GRANT,
-        cost_estimate=pl.CostEstimate(flops=4 * 10**6, bytes_accessed=4 * 2**20, transcendentals=0),
+        cost_estimate=pl.CostEstimate(flops=4000000000, bytes_accessed=4 * 2**20, transcendentals=0),
         name="main",
     )(remapped)
+    relayed = pl.pallas_call(
+        relay_kernel,
+        out_shape=edge,
+        in_specs=[VMEM, ANY],
+        out_specs=VMEM,
+        compiler_params=GRANT,
+        name="relay",
+    )(relayed, part)
+    below = lax.ppermute(relayed, "rad", [(i + 2, i + 1) for i in odd])
     return pl.pallas_call(
         functools.partial(finish_kernel, radii),
         out_shape=whole,
-        in_specs=[ANY, VMEM, VMEM, VMEM, VMEM],
+        in_specs=[ANY, VMEM, VMEM, VMEM, VMEM, VMEM],
         out_specs=ANY,
         scratch_shapes=[
             pltpu.VMEM((changed, 2, height, width), F32),
@@ -234,7 +250,7 @@
         input_output_aliases={0: 0},
         compiler_params=GRANT,
         name="finish",
-    )(settled, remapped, part, far, chip)
+    )(settled, remapped, part, below, chip, above)
 
 
 def solution(mesh):

time: 60.9 us -> 60.4 us (level)
  starting transfers between devices: 7.64 us -> 6.96 us
    ppermute x1 -> x3, starting transfers between devices: 7.55 us -> 6.87 us  [the longest x1 4.9 us: on_device(): relayed = lax.ppermute(far, 'rad', [(i, i + 2) for i in odd])]
    ppermute x1 -> x3, waiting for transfers between devices: 3.12 us -> 3.12 us  [the longest x1 2.46 us: on_device(): above = lax.ppermute(far, 'rad', [(i + 1, i) for i in odd])]
  transfers between devices with their start and end apart: 2 -> 4, of which waited for: 1 -> 2; matrix products, arithmetic and copies ran while one was open for 0% -> 0% of each run, Pallas kernels for 2% -> 3%
where the time goes in v5:
time: 60.4 us; the launch traced here: 60.1 us
  blocking collectives  45.9 us (76%)
  starting transfers between devices  6.96 us (12%)
  Pallas kernels  3.97 us (7%)
  waiting for transfers between devices  3.15 us (5%)
    all_to_all x1, blocking collectives, on_device(): lax.all_to_all(state.reshape(count, height, width), 'az', 0, 0, tiled=True)  26.1 us
    all_to_all x1, blocking collectives, on_device(): lax.all_to_all(moved, 'az', 0, 0, tiled=True)  19.9 us
    ppermute x1, starting transfers between devices, on_device(): relayed = lax.ppermute(far, 'rad', [(i, i + 2) for i in odd])  4.9 us
    ppermute x1, waiting for transfers between devices, on_device(): above = lax.ppermute(far, 'rad', [(i + 1, i) for i in odd])  2.46 us
    pallas_call x1, Pallas kernels, on_device(): pl.pallas_call(remap_kernel, out_shape=jax.ShapeDtypeStruct((count * (hei...  1.59 us
    pallas_call x1, Pallas kernels, on_device(): pl.pallas_call(main_kernel, out_shape=(whole, jax.ShapeDtypeStruct((chang...  1.51 us
    ppermute x1, starting transfers between devices, on_device(): above = lax.ppermute(far, 'rad', [(i + 1, i) for i in odd])  1.29 us
  transfers between devices with their start and end apart: 4, of which 2 were waited for; matrix products, arithmetic and copies ran while one was open for 0% of the time, Pallas kernels for 3%

profile of v5, /device:TPU:1, one launch (start us, length us, event | category | flops | bytes accessed | tf_op | source)
XLA Modules:
  0.0 60.1 jit_solution(7400960211775703297)
XLA Ops:
  0.0 0.0 copy-start.1
  0.0 0.0 copy-start
  0.0 26.1 %all_to_all.10.x_ref = f32[32,64,128]{2,1,0:T(8,128)S(1)} all-to-all(f32[32,64,128]{2,1,0:T(8,128)} %bitcast.7), channel_id=1, replica_groups=mesh['az'=32,'rad'=8] {'az'}, dimensions={0} | all-to-all | bytes 2097152 | tf_op jit(solution)/shard_map/all_to_all | solution.py:191
  26.1 0.0 copy-done.1
  26.1 0.0 copy-done
  26.1 1.6 %remap.1 = f32[2080,128]{1,0:T(8,128)S(1)} custom-call(s32[4]{0:T(128)S(1)} %copy-done, f32[4]{0:T(128)S(1)} %copy-done.1, f32[32,64,128]{2,1,0:T(8,128)S(1)} %all_to_all.10.x_ref), custom_call_target="tpu_custom_call" | custom-call | tf_op jit(solution)/shard_map/remap/pallas_call | solution.py:192
  27.7 19.9 %all_to_all.11 = f32[32,65,1,128]{3,2,1,0:T(1,128)S(1)} all-to-all(f32[32,65,1,128]{3,2,1,0:T(1,128)S(1)} %bitcast.6), channel_id=1, replica_groups=mesh['az'=32,'rad'=8] {'az'}, dimensions={0} | all-to-all | bytes 2129920 | tf_op jit(solution)/shard_map/all_to_all | solution.py:202
  47.6 1.3 %collective-permute-start.3 = (f32[5,64,128]{2,1,0:T(8,128)S(1)}, f32[5,64,128]{2,1,0:T(8,128)S(1)}, u32[]{:S(2)}, u32[]{:S(2)}) collective-permute-start(f32[5,64,128]{2,1,0:T(8,128)S(1)} %get-tuple-element.11), channel_id=1, source_target_pairs={{2,1},{4,3},{6,5},{10,9},{12,11},{14,13},{18,17},{20,19},{22,21},{... | collective-permute-start | bytes 491528 | tf_op jit(solution)/shard_map/ppermute | solution.py:214
  48.9 4.9 %collective-permute-start = (f32[5,64,128]{2,1,0:T(8,128)S(1)}, f32[5,64,128]{2,1,0:T(8,128)S(1)}, u32[]{:S(2)}, u32[]{:S(2)}) collective-permute-start(f32[5,64,128]{2,1,0:T(8,128)S(1)} %get-tuple-element.11), channel_id=1, source_target_pairs={{1,3},{3,5},{5,7},{9,11},{11,13},{13,15},{17,19},{19,21},{21,23},{... | collective-permute-start | bytes 491528 | tf_op jit(solution)/shard_map/ppermute | solution.py:213
  53.8 1.5 %main.1 = (f32[8,4,64,128]{3,2,1,0:T(8,128)}, f32[5,2,64,128]{3,2,1,0:T(8,128)S(1)}) custom-call(f32[2080,128]{1,0:T(8,128)S(1)} %bitcast.4), custom_call_target="tpu_custom_call" | custom-call | flops 4000000000 | bytes 4194304 | tf_op jit(solution)/shard_map/main/pallas_call | solution.py:218
  55.3 0.1 collective-permute-start.2
  55.4 0.7 %collective-permute-done.from_ref = f32[5,64,128]{2,1,0:T(8,128)S(1)} collective-permute-done((f32[5,64,128]{2,1,0:T(8,128)S(1)}, f32[5,64,128]{2,1,0:T(8,128)S(1)}, u32[]{:S(2)}, u32[]{:S(2)}) %collective-permute-start) | collective-permute-done | bytes 163872 | tf_op jit(solution)/shard_map/ppermute | solution.py:213
  56.1 0.7 %collective-permute-start.1 = (f32[5,64,128]{2,1,0:T(8,128)S(1)}, f32[5,64,128]{2,1,0:T(8,128)S(1)}, u32[]{:S(2)}, u32[]{:S(2)}) collective-permute-start(f32[5,64,128]{2,1,0:T(8,128)S(1)} %relay.1), channel_id=1, source_target_pairs={{3,2},{5,4},{7,6},{11,10},{13,12},{15,14},{19,18},{21,20},{23,22},... | collective-permute-start | bytes 491528 | tf_op jit(solution)/shard_map/ppermute | solution.py:240
  56.8 0.0 collective-permute-done.2.chip_ref
  56.8 2.5 %collective-permute-done.3.above_ref = f32[5,64,128]{2,1,0:T(8,128)S(1)} collective-permute-done((f32[5,64,128]{2,1,0:T(8,128)S(1)}, f32[5,64,128]{2,1,0:T(8,128)S(1)}, u32[]{:S(2)}, u32[]{:S(2)}) %collective-permute-start.3) | collective-permute-done | bytes 163872 | tf_op jit(solution)/shard_map/ppermute | solution.py:214
  59.3 0.0 collective-permute-done.1.below_ref
  59.3 0.8 %finish.1 = f32[8,4,64,128]{3,2,1,0:T(8,128)} custom-call(f32[8,4,64,128]{3,2,1,0:T(8,128)} %get-tuple-element.9.base_ref, f32[2080,128]{1,0:T(8,128)S(1)} %bitcast.5, f32[5,2,64,128]{3,2,1,0:T(8,128)S(1)} %get-tuple-element.10.part_ref, f32[5,64,128]{2,1,0:T(8,128)S(1)} %collective-permute-done.1.below_ref, ...), custom_call_target="tpu_custom_call", output_to_operand_aliasing={{}: (0, {})} | custom-call | tf_op jit(solution)/shard_map/finish/pallas_call | solution.py:241
  (2 shorter events, 0.1 us)
Async XLA Ops:
  0.0 26.1 %copy-start.1 = (f32[4]{0:T(128)S(1)}, f32[4]{0:T(128)}, u32[]{:S(2)}) copy-start(f32[4]{0:T(128)} %fracs_ref.1) | copy-start | bytes 52
  0.0 26.1 %copy-start = (s32[4]{0:T(128)S(1)}, s32[4]{0:T(128)}, u32[]{:S(2)}) copy-start(s32[4]{0:T(128)} %shifts_ref.1) | copy-start | bytes 52
  47.6 11.7 %collective-permute-start.3 = (f32[5,64,128]{2,1,0:T(8,128)S(1)}, f32[5,64,128]{2,1,0:T(8,128)S(1)}, u32[]{:S(2)}, u32[]{:S(2)}) collective-permute-start(f32[5,64,128]{2,1,0:T(8,128)S(1)} %get-tuple-element.11), channel_id=1, source_target_pairs={{2,1},{4,3},{6,5},{10,9},{12,11},{14,13},{18,17},{20,19},{22,21},{... | collective-permute-start | bytes 491528 | tf_op jit(solution)/shard_map/ppermute | solution.py:214
  48.9 7.2 %collective-permute-start = (f32[5,64,128]{2,1,0:T(8,128)S(1)}, f32[5,64,128]{2,1,0:T(8,128)S(1)}, u32[]{:S(2)}, u32[]{:S(2)}) collective-permute-start(f32[5,64,128]{2,1,0:T(8,128)S(1)} %get-tuple-element.11), channel_id=1, source_target_pairs={{1,3},{3,5},{5,7},{9,11},{11,13},{13,15},{17,19},{19,21},{21,23},{... | collective-permute-start | bytes 491528 | tf_op jit(solution)/shard_map/ppermute | solution.py:213
  55.3 1.5 %collective-permute-start.2 = (f32[5,64,128]{2,1,0:T(8,128)S(1)}, f32[5,64,128]{2,1,0:T(8,128)S(1)}, u32[]{:S(2)}, u32[]{:S(2)}) collective-permute-start(f32[5,64,128]{2,1,0:T(8,128)S(1)} %get-tuple-element.12), channel_id=1, source_target_pairs={{0,1},{1,0},{2,3},{3,2},{4,5},{5,4},{6,7},{7,6},{8,9},{9,8},{10,11... | collective-permute-start | bytes 491528 | tf_op jit(solution)/shard_map/ppermute | solution.py:215
  56.1 3.2 %collective-permute-start.1 = (f32[5,64,128]{2,1,0:T(8,128)S(1)}, f32[5,64,128]{2,1,0:T(8,128)S(1)}, u32[]{:S(2)}, u32[]{:S(2)}) collective-permute-start(f32[5,64,128]{2,1,0:T(8,128)S(1)} %relay.1), channel_id=1, source_target_pairs={{3,2},{5,4},{7,6},{11,10},{13,12},{15,14},{19,18},{21,20},{23,22},... | collective-permute-start | bytes 491528 | tf_op jit(solution)/shard_map/ppermute | solution.py:240

commit v6 on v5

--- a/solution.py
+++ b/solution.py
@@ -175,9 +175,15 @@
         wy, wz, fx, es, pm = halo
         vx = slab(s_ref, radii + r, height)
         changes = (-fx, -pm, -wz, wy, -(vx * es))
-        for at, v in enumerate(EDGE_CHANGED):
-            done_ref[at, pair] = part_ref[at, pair] + changes[at]
-            copy = pltpu.make_async_copy(done_ref.at[at, pair], o_ref.at[v, r], sems.at[at, pair])
+        for group, (begin, end) in enumerate(((0, 2), (2, 5))):
+            for at in range(begin, end):
+                done_ref[pair, at] = part_ref[at, pair] + changes[at]
+            first = EDGE_CHANGED[begin]
+            copy = pltpu.make_async_copy(
+                done_ref.at[pair, begin:end],
+                o_ref.at[first : first + end - begin, r],
+                sems.at[group, pair],
+            )
             copy.start()
             copies.append(copy)
     for copy in copies:
@@ -244,8 +250,8 @@
         in_specs=[ANY, VMEM, VMEM, VMEM, VMEM, VMEM],
         out_specs=ANY,
         scratch_shapes=[
-            pltpu.VMEM((changed, 2, height, width), F32),
-            pltpu.SemaphoreType.DMA((changed, 2)),
+            pltpu.VMEM((2, changed, height, width), F32),
+            pltpu.SemaphoreType.DMA((2, 2)),
         ],
         input_output_aliases={0: 0},
         compiler_params=GRANT,

time: 60.4 us -> 60.3 us (level)
  no operation moved by 1% of the time
where the time goes in v6:
time: 60.3 us; the launch traced here: 60 us
  blocking collectives  45.9 us (76%)
  starting transfers between devices  6.96 us (12%)
  Pallas kernels  3.93 us (7%)
  waiting for transfers between devices  3.15 us (5%)
    all_to_all x1, blocking collectives, on_device(): lax.all_to_all(state.reshape(count, height, width), 'az', 0, 0, tiled=True)  26.1 us
    all_to_all x1, blocking collectives, on_device(): lax.all_to_all(moved, 'az', 0, 0, tiled=True)  19.9 us
    ppermute x1, starting transfers between devices, on_device(): relayed = lax.ppermute(far, 'rad', [(i, i + 2) for i in odd])  4.9 us
    ppermute x1, waiting for transfers between devices, on_device(): above = lax.ppermute(far, 'rad', [(i + 1, i) for i in odd])  2.46 us
    pallas_call x1, Pallas kernels, on_device(): pl.pallas_call(remap_kernel, out_shape=jax.ShapeDtypeStruct((count * (hei...  1.59 us
    pallas_call x1, Pallas kernels, on_device(): pl.pallas_call(main_kernel, out_shape=(whole, jax.ShapeDtypeStruct((chang...  1.51 us
    ppermute x1, starting transfers between devices, on_device(): above = lax.ppermute(far, 'rad', [(i + 1, i) for i in odd])  1.29 us
  transfers between devices with their start and end apart: 4, of which 2 were waited for; matrix products, arithmetic and copies ran while one was open for 0% of the time, Pallas kernels for 3%

profile of v6, /device:TPU:1, one launch (start us, length us, event | category | flops | bytes accessed | tf_op | source)
XLA Modules:
  0.0 60.0 jit_solution(2740099523413537430)
XLA Ops:
  0.0 0.0 copy-start.1
  0.0 0.0 copy-start
  0.0 26.1 %all_to_all.10.x_ref = f32[32,64,128]{2,1,0:T(8,128)S(1)} all-to-all(f32[32,64,128]{2,1,0:T(8,128)} %bitcast.7), channel_id=1, replica_groups=mesh['az'=32,'rad'=8] {'az'}, dimensions={0} | all-to-all | bytes 2097152 | tf_op jit(solution)/shard_map/all_to_all | solution.py:197
  26.1 0.0 copy-done.1
  26.1 0.0 copy-done
  26.1 1.6 %remap.1 = f32[2080,128]{1,0:T(8,128)S(1)} custom-call(s32[4]{0:T(128)S(1)} %copy-done, f32[4]{0:T(128)S(1)} %copy-done.1, f32[32,64,128]{2,1,0:T(8,128)S(1)} %all_to_all.10.x_ref), custom_call_target="tpu_custom_call" | custom-call | tf_op jit(solution)/shard_map/remap/pallas_call | solution.py:198
  27.7 19.9 %all_to_all.11 = f32[32,65,1,128]{3,2,1,0:T(1,128)S(1)} all-to-all(f32[32,65,1,128]{3,2,1,0:T(1,128)S(1)} %bitcast.6), channel_id=1, replica_groups=mesh['az'=32,'rad'=8] {'az'}, dimensions={0} | all-to-all | bytes 2129920 | tf_op jit(solution)/shard_map/all_to_all | solution.py:208
  47.6 1.3 %collective-permute-start.3 = (f32[5,64,128]{2,1,0:T(8,128)S(1)}, f32[5,64,128]{2,1,0:T(8,128)S(1)}, u32[]{:S(2)}, u32[]{:S(2)}) collective-permute-start(f32[5,64,128]{2,1,0:T(8,128)S(1)} %get-tuple-element.11), channel_id=1, source_target_pairs={{2,1},{4,3},{6,5},{10,9},{12,11},{14,13},{18,17},{20,19},{22,21},{... | collective-permute-start | bytes 491528 | tf_op jit(solution)/shard_map/ppermute | solution.py:220
  48.9 4.9 %collective-permute-start = (f32[5,64,128]{2,1,0:T(8,128)S(1)}, f32[5,64,128]{2,1,0:T(8,128)S(1)}, u32[]{:S(2)}, u32[]{:S(2)}) collective-permute-start(f32[5,64,128]{2,1,0:T(8,128)S(1)} %get-tuple-element.11), channel_id=1, source_target_pairs={{1,3},{3,5},{5,7},{9,11},{11,13},{13,15},{17,19},{19,21},{21,23},{... | collective-permute-start | bytes 491528 | tf_op jit(solution)/shard_map/ppermute | solution.py:219
  53.8 1.5 %main.1 = (f32[8,4,64,128]{3,2,1,0:T(8,128)}, f32[5,2,64,128]{3,2,1,0:T(8,128)S(1)}) custom-call(f32[2080,128]{1,0:T(8,128)S(1)} %bitcast.4), custom_call_target="tpu_custom_call" | custom-call | flops 4000000000 | bytes 4194304 | tf_op jit(solution)/shard_map/main/pallas_call | solution.py:224
  55.3 0.1 collective-permute-start.2
  55.4 0.7 %collective-permute-done.from_ref = f32[5,64,128]{2,1,0:T(8,128)S(1)} collective-permute-done((f32[5,64,128]{2,1,0:T(8,128)S(1)}, f32[5,64,128]{2,1,0:T(8,128)S(1)}, u32[]{:S(2)}, u32[]{:S(2)}) %collective-permute-start) | collective-permute-done | bytes 163872 | tf_op jit(solution)/shard_map/ppermute | solution.py:219
  56.1 0.7 %collective-permute-start.1 = (f32[5,64,128]{2,1,0:T(8,128)S(1)}, f32[5,64,128]{2,1,0:T(8,128)S(1)}, u32[]{:S(2)}, u32[]{:S(2)}) collective-permute-start(f32[5,64,128]{2,1,0:T(8,128)S(1)} %relay.1), channel_id=1, source_target_pairs={{3,2},{5,4},{7,6},{11,10},{13,12},{15,14},{19,18},{21,20},{23,22},... | collective-permute-start | bytes 491528 | tf_op jit(solution)/shard_map/ppermute | solution.py:246
  56.8 0.0 collective-permute-done.2.chip_ref
  56.8 2.5 %collective-permute-done.3.above_ref = f32[5,64,128]{2,1,0:T(8,128)S(1)} collective-permute-done((f32[5,64,128]{2,1,0:T(8,128)S(1)}, f32[5,64,128]{2,1,0:T(8,128)S(1)}, u32[]{:S(2)}, u32[]{:S(2)}) %collective-permute-start.3) | collective-permute-done | bytes 163872 | tf_op jit(solution)/shard_map/ppermute | solution.py:220
  59.3 0.0 collective-permute-done.1.below_ref
  59.3 0.8 %finish.1 = f32[8,4,64,128]{3,2,1,0:T(8,128)} custom-call(f32[8,4,64,128]{3,2,1,0:T(8,128)} %get-tuple-element.9.base_ref, f32[2080,128]{1,0:T(8,128)S(1)} %bitcast.5, f32[5,2,64,128]{3,2,1,0:T(8,128)S(1)} %get-tuple-element.10.part_ref, f32[5,64,128]{2,1,0:T(8,128)S(1)} %collective-permute-done.1.below_ref, ...), custom_call_target="tpu_custom_call", output_to_operand_aliasing={{}: (0, {})} | custom-call | tf_op jit(solution)/shard_map/finish/pallas_call | solution.py:247
  (2 shorter events, 0.1 us)
Async XLA Ops:
  0.0 26.1 %copy-start.1 = (f32[4]{0:T(128)S(1)}, f32[4]{0:T(128)}, u32[]{:S(2)}) copy-start(f32[4]{0:T(128)} %fracs_ref.1) | copy-start | bytes 52
  0.0 26.1 %copy-start = (s32[4]{0:T(128)S(1)}, s32[4]{0:T(128)}, u32[]{:S(2)}) copy-start(s32[4]{0:T(128)} %shifts_ref.1) | copy-start | bytes 52
  47.6 11.7 %collective-permute-start.3 = (f32[5,64,128]{2,1,0:T(8,128)S(1)}, f32[5,64,128]{2,1,0:T(8,128)S(1)}, u32[]{:S(2)}, u32[]{:S(2)}) collective-permute-start(f32[5,64,128]{2,1,0:T(8,128)S(1)} %get-tuple-element.11), channel_id=1, source_target_pairs={{2,1},{4,3},{6,5},{10,9},{12,11},{14,13},{18,17},{20,19},{22,21},{... | collective-permute-start | bytes 491528 | tf_op jit(solution)/shard_map/ppermute | solution.py:220
  48.9 7.2 %collective-permute-start = (f32[5,64,128]{2,1,0:T(8,128)S(1)}, f32[5,64,128]{2,1,0:T(8,128)S(1)}, u32[]{:S(2)}, u32[]{:S(2)}) collective-permute-start(f32[5,64,128]{2,1,0:T(8,128)S(1)} %get-tuple-element.11), channel_id=1, source_target_pairs={{1,3},{3,5},{5,7},{9,11},{11,13},{13,15},{17,19},{19,21},{21,23},{... | collective-permute-start | bytes 491528 | tf_op jit(solution)/shard_map/ppermute | solution.py:219
  55.3 1.5 %collective-permute-start.2 = (f32[5,64,128]{2,1,0:T(8,128)S(1)}, f32[5,64,128]{2,1,0:T(8,128)S(1)}, u32[]{:S(2)}, u32[]{:S(2)}) collective-permute-start(f32[5,64,128]{2,1,0:T(8,128)S(1)} %get-tuple-element.12), channel_id=1, source_target_pairs={{0,1},{1,0},{2,3},{3,2},{4,5},{5,4},{6,7},{7,6},{8,9},{9,8},{10,11... | collective-permute-start | bytes 491528 | tf_op jit(solution)/shard_map/ppermute | solution.py:221
  56.1 3.2 %collective-permute-start.1 = (f32[5,64,128]{2,1,0:T(8,128)S(1)}, f32[5,64,128]{2,1,0:T(8,128)S(1)}, u32[]{:S(2)}, u32[]{:S(2)}) collective-permute-start(f32[5,64,128]{2,1,0:T(8,128)S(1)} %relay.1), channel_id=1, source_target_pairs={{3,2},{5,4},{7,6},{11,10},{13,12},{15,14},{19,18},{21,20},{23,22},... | collective-permute-start | bytes 491528 | tf_op jit(solution)/shard_map/ppermute | solution.py:246

commit v7 on v6

--- a/solution.py
+++ b/solution.py
@@ -27,6 +27,7 @@
     frac = fracs_ref[mine]
     block_shift = lax.div(shift, width)
     lane_shift = lax.rem(shift, width)
+    next_shift = lax.rem(lane_shift + 1, width)
     lane = lax.broadcasted_iota(jnp.int32, (height, width), 1)
     own = lane + lane_shift < width
     own_next = lane + lane_shift + 1 < width
@@ -34,7 +35,7 @@
         near = x_ref[lax.rem(i - block_shift + blocks, blocks)]
         far = x_ref[lax.rem(i - block_shift - 1 + 2 * blocks, blocks)]
         first = pltpu.roll(jnp.where(own, near, far), lane_shift, 1)
-        second = pltpu.roll(jnp.where(own_next, near, far), lane_shift + 1, 1)
+        second = pltpu.roll(jnp.where(own_next, near, far), next_shift, 1)
         o_ref[tall * i : tall * i + height, :] = (1.0 - frac) * first + frac * second
     pair = lax.shift_right_logical(lane, 1)
     ends = jnp.zeros((height, width), F32)

time: 60.3 us -> 60.3 us (level)
  no operation moved by 1% of the time
where the time goes in v7:
time: 60.3 us; the launch traced here: 60 us
  blocking collectives  45.9 us (76%)
  starting transfers between devices  6.96 us (12%)
  Pallas kernels  3.93 us (7%)
  waiting for transfers between devices  3.15 us (5%)
    all_to_all x1, blocking collectives, on_device(): lax.all_to_all(state.reshape(count, height, width), 'az', 0, 0, tiled=True)  26.1 us
    all_to_all x1, blocking collectives, on_device(): lax.all_to_all(moved, 'az', 0, 0, tiled=True)  19.9 us
    ppermute x1, starting transfers between devices, on_device(): relayed = lax.ppermute(far, 'rad', [(i, i + 2) for i in odd])  4.9 us
    ppermute x1, waiting for transfers between devices, on_device(): above = lax.ppermute(far, 'rad', [(i + 1, i) for i in odd])  2.46 us
    pallas_call x1, Pallas kernels, on_device(): pl.pallas_call(remap_kernel, out_shape=jax.ShapeDtypeStruct((count * (hei...  1.59 us
    pallas_call x1, Pallas kernels, on_device(): pl.pallas_call(main_kernel, out_shape=(whole, jax.ShapeDtypeStruct((chang...  1.51 us
    ppermute x1, starting transfers between devices, on_device(): above = lax.ppermute(far, 'rad', [(i + 1, i) for i in odd])  1.29 us
  transfers between devices with their start and end apart: 4, of which 2 were waited for; matrix products, arithmetic and copies ran while one was open for 0% of the time, Pallas kernels for 3%

profile of v7, /device:TPU:1, one launch (start us, length us, event | category | flops | bytes accessed | tf_op | source)
XLA Modules:
  0.0 60.0 jit_solution(17288765024504945529)
XLA Ops:
  0.0 0.0 copy-start.1
  0.0 0.0 copy-start
  0.0 26.1 %all_to_all.10.x_ref = f32[32,64,128]{2,1,0:T(8,128)S(1)} all-to-all(f32[32,64,128]{2,1,0:T(8,128)} %bitcast.7), channel_id=1, replica_groups=mesh['az'=32,'rad'=8] {'az'}, dimensions={0} | all-to-all | bytes 2097152 | tf_op jit(solution)/shard_map/all_to_all | solution.py:198
  26.1 0.0 copy-done.1
  26.1 0.0 copy-done
  26.1 1.6 %remap.1 = f32[2080,128]{1,0:T(8,128)S(1)} custom-call(s32[4]{0:T(128)S(1)} %copy-done, f32[4]{0:T(128)S(1)} %copy-done.1, f32[32,64,128]{2,1,0:T(8,128)S(1)} %all_to_all.10.x_ref), custom_call_target="tpu_custom_call" | custom-call | tf_op jit(solution)/shard_map/remap/pallas_call | solution.py:199
  27.7 19.9 %all_to_all.11 = f32[32,65,1,128]{3,2,1,0:T(1,128)S(1)} all-to-all(f32[32,65,1,128]{3,2,1,0:T(1,128)S(1)} %bitcast.6), channel_id=1, replica_groups=mesh['az'=32,'rad'=8] {'az'}, dimensions={0} | all-to-all | bytes 2129920 | tf_op jit(solution)/shard_map/all_to_all | solution.py:209
  47.6 1.3 %collective-permute-start.3 = (f32[5,64,128]{2,1,0:T(8,128)S(1)}, f32[5,64,128]{2,1,0:T(8,128)S(1)}, u32[]{:S(2)}, u32[]{:S(2)}) collective-permute-start(f32[5,64,128]{2,1,0:T(8,128)S(1)} %get-tuple-element.11), channel_id=1, source_target_pairs={{2,1},{4,3},{6,5},{10,9},{12,11},{14,13},{18,17},{20,19},{22,21},{... | collective-permute-start | bytes 491528 | tf_op jit(solution)/shard_map/ppermute | solution.py:221
  48.9 4.9 %collective-permute-start = (f32[5,64,128]{2,1,0:T(8,128)S(1)}, f32[5,64,128]{2,1,0:T(8,128)S(1)}, u32[]{:S(2)}, u32[]{:S(2)}) collective-permute-start(f32[5,64,128]{2,1,0:T(8,128)S(1)} %get-tuple-element.11), channel_id=1, source_target_pairs={{1,3},{3,5},{5,7},{9,11},{11,13},{13,15},{17,19},{19,21},{21,23},{... | collective-permute-start | bytes 491528 | tf_op jit(solution)/shard_map/ppermute | solution.py:220
  53.8 1.5 %main.1 = (f32[8,4,64,128]{3,2,1,0:T(8,128)}, f32[5,2,64,128]{3,2,1,0:T(8,128)S(1)}) custom-call(f32[2080,128]{1,0:T(8,128)S(1)} %bitcast.4), custom_call_target="tpu_custom_call" | custom-call | flops 4000000000 | bytes 4194304 | tf_op jit(solution)/shard_map/main/pallas_call | solution.py:225
  55.3 0.1 collective-permute-start.2
  55.4 0.7 %collective-permute-done.from_ref = f32[5,64,128]{2,1,0:T(8,128)S(1)} collective-permute-done((f32[5,64,128]{2,1,0:T(8,128)S(1)}, f32[5,64,128]{2,1,0:T(8,128)S(1)}, u32[]{:S(2)}, u32[]{:S(2)}) %collective-permute-start) | collective-permute-done | bytes 163872 | tf_op jit(solution)/shard_map/ppermute | solution.py:220
  56.1 0.7 %collective-permute-start.1 = (f32[5,64,128]{2,1,0:T(8,128)S(1)}, f32[5,64,128]{2,1,0:T(8,128)S(1)}, u32[]{:S(2)}, u32[]{:S(2)}) collective-permute-start(f32[5,64,128]{2,1,0:T(8,128)S(1)} %relay.1), channel_id=1, source_target_pairs={{3,2},{5,4},{7,6},{11,10},{13,12},{15,14},{19,18},{21,20},{23,22},... | collective-permute-start | bytes 491528 | tf_op jit(solution)/shard_map/ppermute | solution.py:247
  56.8 0.0 collective-permute-done.2.chip_ref
  56.8 2.5 %collective-permute-done.3.above_ref = f32[5,64,128]{2,1,0:T(8,128)S(1)} collective-permute-done((f32[5,64,128]{2,1,0:T(8,128)S(1)}, f32[5,64,128]{2,1,0:T(8,128)S(1)}, u32[]{:S(2)}, u32[]{:S(2)}) %collective-permute-start.3) | collective-permute-done | bytes 163872 | tf_op jit(solution)/shard_map/ppermute | solution.py:221
  59.3 0.0 collective-permute-done.1.below_ref
  59.3 0.8 %finish.1 = f32[8,4,64,128]{3,2,1,0:T(8,128)} custom-call(f32[8,4,64,128]{3,2,1,0:T(8,128)} %get-tuple-element.9.base_ref, f32[2080,128]{1,0:T(8,128)S(1)} %bitcast.5, f32[5,2,64,128]{3,2,1,0:T(8,128)S(1)} %get-tuple-element.10.part_ref, f32[5,64,128]{2,1,0:T(8,128)S(1)} %collective-permute-done.1.below_ref, ...), custom_call_target="tpu_custom_call", output_to_operand_aliasing={{}: (0, {})} | custom-call | tf_op jit(solution)/shard_map/finish/pallas_call | solution.py:248
  (2 shorter events, 0.1 us)
Async XLA Ops:
  0.0 26.1 %copy-start.1 = (f32[4]{0:T(128)S(1)}, f32[4]{0:T(128)}, u32[]{:S(2)}) copy-start(f32[4]{0:T(128)} %fracs_ref.1) | copy-start | bytes 52
  0.0 26.1 %copy-start = (s32[4]{0:T(128)S(1)}, s32[4]{0:T(128)}, u32[]{:S(2)}) copy-start(s32[4]{0:T(128)} %shifts_ref.1) | copy-start | bytes 52
  47.6 11.7 %collective-permute-start.3 = (f32[5,64,128]{2,1,0:T(8,128)S(1)}, f32[5,64,128]{2,1,0:T(8,128)S(1)}, u32[]{:S(2)}, u32[]{:S(2)}) collective-permute-start(f32[5,64,128]{2,1,0:T(8,128)S(1)} %get-tuple-element.11), channel_id=1, source_target_pairs={{2,1},{4,3},{6,5},{10,9},{12,11},{14,13},{18,17},{20,19},{22,21},{... | collective-permute-start | bytes 491528 | tf_op jit(solution)/shard_map/ppermute | solution.py:221
  48.9 7.2 %collective-permute-start = (f32[5,64,128]{2,1,0:T(8,128)S(1)}, f32[5,64,128]{2,1,0:T(8,128)S(1)}, u32[]{:S(2)}, u32[]{:S(2)}) collective-permute-start(f32[5,64,128]{2,1,0:T(8,128)S(1)} %get-tuple-element.11), channel_id=1, source_target_pairs={{1,3},{3,5},{5,7},{9,11},{11,13},{13,15},{17,19},{19,21},{21,23},{... | collective-permute-start | bytes 491528 | tf_op jit(solution)/shard_map/ppermute | solution.py:220
  55.3 1.5 %collective-permute-start.2 = (f32[5,64,128]{2,1,0:T(8,128)S(1)}, f32[5,64,128]{2,1,0:T(8,128)S(1)}, u32[]{:S(2)}, u32[]{:S(2)}) collective-permute-start(f32[5,64,128]{2,1,0:T(8,128)S(1)} %get-tuple-element.12), channel_id=1, source_target_pairs={{0,1},{1,0},{2,3},{3,2},{4,5},{5,4},{6,7},{7,6},{8,9},{9,8},{10,11... | collective-permute-start | bytes 491528 | tf_op jit(solution)/shard_map/ppermute | solution.py:222
  56.1 3.2 %collective-permute-start.1 = (f32[5,64,128]{2,1,0:T(8,128)S(1)}, f32[5,64,128]{2,1,0:T(8,128)S(1)}, u32[]{:S(2)}, u32[]{:S(2)}) collective-permute-start(f32[5,64,128]{2,1,0:T(8,128)S(1)} %relay.1), channel_id=1, source_target_pairs={{3,2},{5,4},{7,6},{11,10},{13,12},{15,14},{19,18},{21,20},{23,22},... | collective-permute-start | bytes 491528 | tf_op jit(solution)/shard_map/ppermute | solution.py:247

commit v8 on v4

--- a/solution.py
+++ b/solution.py
@@ -27,6 +27,7 @@
     frac = fracs_ref[mine]
     block_shift = lax.div(shift, width)
     lane_shift = lax.rem(shift, width)
+    next_shift = lax.rem(lane_shift + 1, width)
     lane = lax.broadcasted_iota(jnp.int32, (height, width), 1)
     own = lane + lane_shift < width
     own_next = lane + lane_shift + 1 < width
@@ -34,7 +35,7 @@
         near = x_ref[lax.rem(i - block_shift + blocks, blocks)]
         far = x_ref[lax.rem(i - block_shift - 1 + 2 * blocks, blocks)]
         first = pltpu.roll(jnp.where(own, near, far), lane_shift, 1)
-        second = pltpu.roll(jnp.where(own_next, near, far), lane_shift + 1, 1)
+        second = pltpu.roll(jnp.where(own_next, near, far), next_shift, 1)
         o_ref[tall * i : tall * i + height, :] = (1.0 - frac) * first + frac * second
     pair = lax.shift_right_logical(lane, 1)
     ends = jnp.zeros((height, width), F32)
@@ -154,28 +155,44 @@
         copy.wait()
 
 
-def finish_kernel(radii, base_ref, s_ref, part_ref, far_ref, chip_ref, o_ref, done_ref, sems):
-    del base_ref
-    height = chip_ref.shape[1]
-    odd = lax.rem(lax.axis_index("rad"), 2) == 1
+def add_halo(radii, outward, halo_refs, s_ref, part_ref, o_ref, done_ref, sems):
+    height = done_ref.shape[1]
+    odd = lax.rem(lax.axis_index("rad"), 2)
+    pair = odd if outward else 1 - odd
+    upper = pair == 1
+    step = jnp.where(upper, 0.1, -0.1)
+    below_ref, above_ref = halo_refs
+    wy, wz, fx, es, pm = [
+        step * (below_ref[at] if below_ref is above_ref else jnp.where(upper, above_ref[at], below_ref[at]))
+        for at in range(len(EDGE_FIELDS))
+    ]
+    vx = jnp.where(upper, slab(s_ref, 2 * radii - 1, height), slab(s_ref, radii, height))
+    changes = (-fx, -pm, -wz, wy, -(vx * es))
     copies = []
-    for pair in range(2):
-        r = pair * (radii - 1)
-        step = 0.1 if pair else -0.1
-        halo = []
-        for at in range(len(EDGE_FIELDS)):
-            up, down = (far_ref, chip_ref) if pair else (chip_ref, far_ref)
-            halo.append(step * jnp.where(odd, up[at], down[at]))
-        wy, wz, fx, es, pm = halo
-        vx = slab(s_ref, radii + r, height)
-        changes = (-fx, -pm, -wz, wy, -(vx * es))
-        for at, v in enumerate(EDGE_CHANGED):
-            done_ref[at, pair] = part_ref[at, pair] + changes[at]
-            copy = pltpu.make_async_copy(done_ref.at[at, pair], o_ref.at[v, r], sems.at[at, pair])
-            copy.start()
-            copies.append(copy)
+    for group, (begin, end) in enumerate(((0, 2), (2, 5))):
+        for at in range(begin, end):
+            done_ref[at] = part_ref[at, pair] + changes[at]
+        first = EDGE_CHANGED[begin]
+        copy = pltpu.make_async_copy(
+            done_ref.at[begin:end],
+            o_ref.at[first : first + end - begin, pair * (radii - 1)],
+            sems.at[group],
+        )
+        copy.start()
+        copies.append(copy)
     for copy in copies:
         copy.wait()
+
+
+def relay_kernel(radii, from_ref, base_ref, s_ref, part_ref, chip_ref, to_ref, o_ref, done_ref, sems):
+    del base_ref
+    to_ref[...] = from_ref[...]
+    add_halo(radii, False, (chip_ref, chip_ref), s_ref, part_ref, o_ref, done_ref, sems)
+
+
+def finish_kernel(radii, base_ref, s_ref, part_ref, below_ref, above_ref, o_ref, done_ref, sems):
+    del base_ref
+    add_halo(radii, True, (below_ref, above_ref), s_ref, part_ref, o_ref, done_ref, sems)
 
 
 def on_device(state, shifts, fracs):
@@ -204,7 +221,8 @@
         name="edges",
     )(remapped)
     odd = range(1, bands - 1, 2)
-    far = lax.ppermute(far, "rad", [(i, i + 1) for i in odd] + [(i + 1, i) for i in odd])
+    relayed = lax.ppermute(far, "rad", [(i, i + 2) for i in odd])
+    above = lax.ppermute(far, "rad", [(i + 1, i) for i in odd])
     chip = lax.ppermute(chip, "rad", [(i, i ^ 1) for i in range(bands)])
     changed = len(EDGE_CHANGED)
     whole = jax.ShapeDtypeStruct(state.shape, F32)
@@ -219,22 +237,31 @@
             pltpu.SemaphoreType.DMA((radii,)),
         ],
         compiler_params=GRANT,
-        cost_estimate=pl.CostEstimate(flops=4 * 10**6, bytes_accessed=4 * 2**20, transcendentals=0),
+        cost_estimate=pl.CostEstimate(flops=4000000000, bytes_accessed=4 * 2**20, transcendentals=0),
         name="main",
     )(remapped)
+    scratch = [pltpu.VMEM((changed, height, width), F32), pltpu.SemaphoreType.DMA((2,))]
+    relayed, settled = pl.pallas_call(
+        functools.partial(relay_kernel, radii),
+        out_shape=(edge, whole),
+        in_specs=[VMEM, ANY, VMEM, VMEM, VMEM],
+        out_specs=(VMEM, ANY),
+        scratch_shapes=scratch,
+        input_output_aliases={1: 1},
+        compiler_params=GRANT,
+        name="relay",
+    )(relayed, settled, remapped, part, chip)
+    below = lax.ppermute(relayed, "rad", [(i + 2, i + 1) for i in odd])
     return pl.pallas_call(
         functools.partial(finish_kernel, radii),
         out_shape=whole,
         in_specs=[ANY, VMEM, VMEM, VMEM, VMEM],
         out_specs=ANY,
-        scratch_shapes=[
-            pltpu.VMEM((changed, 2, height, width), F32),
-            pltpu.SemaphoreType.DMA((changed, 2)),
-        ],
+        scratch_shapes=scratch,
         input_output_aliases={0: 0},
         compiler_params=GRANT,
         name="finish",
-    )(settled, remapped, part, far, chip)
+    )(settled, remapped, part, below, above)
 
 
 def solution(mesh):

time: 60.9 us -> 60.6 us (level)
  starting transfers between devices: 7.64 us -> 6.96 us
  waiting for transfers between devices: 3.12 us -> 2.45 us
    pallas_call x0 -> x1, Pallas kernels: none -> 0.69 us  [on_device(): pl.pallas_call(functools.partial(relay_kernel, radii), out_shape=(edge, w...]
    ppermute x1 -> x3, starting transfers between devices: 7.55 us -> 6.87 us  [the longest x1 4.9 us: on_device(): relayed = lax.ppermute(far, 'rad', [(i, i + 2) for i in odd])]
    ppermute x1 -> x3, waiting for transfers between devices: 3.12 us -> 2.45 us  [the longest x1 1.8 us: on_device(): above = lax.ppermute(far, 'rad', [(i + 1, i) for i in odd])]
  transfers between devices with their start and end apart: 2 -> 4, of which waited for: 1 -> 2; matrix products, arithmetic and copies ran while one was open for 0% -> 0% of each run, Pallas kernels for 2% -> 4%
where the time goes in v8:
time: 60.6 us; the launch traced here: 60 us
  blocking collectives  45.9 us (76%)
  starting transfers between devices  6.96 us (11%)
  Pallas kernels  4.54 us (7%)
  waiting for transfers between devices  2.45 us (4%)
    all_to_all x1, blocking collectives, on_device(): lax.all_to_all(state.reshape(count, height, width), 'az', 0, 0, tiled=True)  26.1 us
    all_to_all x1, blocking collectives, on_device(): lax.all_to_all(moved, 'az', 0, 0, tiled=True)  19.9 us
    ppermute x1, starting transfers between devices, on_device(): relayed = lax.ppermute(far, 'rad', [(i, i + 2) for i in odd])  4.9 us
    ppermute x1, waiting for transfers between devices, on_device(): above = lax.ppermute(far, 'rad', [(i + 1, i) for i in odd])  1.8 us
    pallas_call x1, Pallas kernels, on_device(): pl.pallas_call(remap_kernel, out_shape=jax.ShapeDtypeStruct((count * (hei...  1.59 us
    pallas_call x1, Pallas kernels, on_device(): pl.pallas_call(main_kernel, out_shape=(whole, jax.ShapeDtypeStruct((chang...  1.51 us
    ppermute x1, starting transfers between devices, on_device(): above = lax.ppermute(far, 'rad', [(i + 1, i) for i in odd])  1.29 us
  transfers between devices with their start and end apart: 4, of which 2 were waited for; matrix products, arithmetic and copies ran while one was open for 0% of the time, Pallas kernels for 4%

profile of v8, /device:TPU:1, one launch (start us, length us, event | category | flops | bytes accessed | tf_op | source)
XLA Modules:
  0.0 60.0 jit_solution(4155478914682537589)
XLA Ops:
  0.0 0.0 copy-start.1
  0.0 0.0 copy-start
  0.0 26.1 %all_to_all.10.x_ref = f32[32,64,128]{2,1,0:T(8,128)S(1)} all-to-all(f32[32,64,128]{2,1,0:T(8,128)} %bitcast.8), channel_id=1, replica_groups=mesh['az'=32,'rad'=8] {'az'}, dimensions={0} | all-to-all | bytes 2097152 | tf_op jit(solution)/shard_map/all_to_all | solution.py:202
  26.1 0.0 copy-done.1
  26.1 0.0 copy-done
  26.1 1.6 %remap.1 = f32[2080,128]{1,0:T(8,128)S(1)} custom-call(s32[4]{0:T(128)S(1)} %copy-done, f32[4]{0:T(128)S(1)} %copy-done.1, f32[32,64,128]{2,1,0:T(8,128)S(1)} %all_to_all.10.x_ref), custom_call_target="tpu_custom_call" | custom-call | tf_op jit(solution)/shard_map/remap/pallas_call | solution.py:203
  27.7 19.9 %all_to_all.11 = f32[32,65,1,128]{3,2,1,0:T(1,128)S(1)} all-to-all(f32[32,65,1,128]{3,2,1,0:T(1,128)S(1)} %bitcast.7), channel_id=1, replica_groups=mesh['az'=32,'rad'=8] {'az'}, dimensions={0} | all-to-all | bytes 2129920 | tf_op jit(solution)/shard_map/all_to_all | solution.py:213
  47.6 1.3 %collective-permute-start.3 = (f32[5,64,128]{2,1,0:T(8,128)S(1)}, f32[5,64,128]{2,1,0:T(8,128)S(1)}, u32[]{:S(2)}, u32[]{:S(2)}) collective-permute-start(f32[5,64,128]{2,1,0:T(8,128)S(1)} %get-tuple-element.11), channel_id=1, source_target_pairs={{2,1},{4,3},{6,5},{10,9},{12,11},{14,13},{18,17},{20,19},{22,21},{... | collective-permute-start | bytes 491528 | tf_op jit(solution)/shard_map/ppermute | solution.py:225
  48.9 4.9 %collective-permute-start = (f32[5,64,128]{2,1,0:T(8,128)S(1)}, f32[5,64,128]{2,1,0:T(8,128)S(1)}, u32[]{:S(2)}, u32[]{:S(2)}) collective-permute-start(f32[5,64,128]{2,1,0:T(8,128)S(1)} %get-tuple-element.11), channel_id=1, source_target_pairs={{1,3},{3,5},{5,7},{9,11},{11,13},{13,15},{17,19},{19,21},{21,23},{... | collective-permute-start | bytes 491528 | tf_op jit(solution)/shard_map/ppermute | solution.py:224
  53.8 0.1 collective-permute-start.1
  53.9 1.5 %main.1 = (f32[8,4,64,128]{3,2,1,0:T(8,128)}, f32[5,2,64,128]{3,2,1,0:T(8,128)S(1)}) custom-call(f32[2080,128]{1,0:T(8,128)S(1)} %bitcast.4), custom_call_target="tpu_custom_call" | custom-call | flops 4000000000 | bytes 4194304 | tf_op jit(solution)/shard_map/main/pallas_call | solution.py:229
  55.4 0.0 collective-permute-done.1.chip_ref
  55.4 0.7 %collective-permute-done.from_ref = f32[5,64,128]{2,1,0:T(8,128)S(1)} collective-permute-done((f32[5,64,128]{2,1,0:T(8,128)S(1)}, f32[5,64,128]{2,1,0:T(8,128)S(1)}, u32[]{:S(2)}, u32[]{:S(2)}) %collective-permute-start) | collective-permute-done | bytes 163872 | tf_op jit(solution)/shard_map/ppermute | solution.py:224
  56.1 0.7 %relay.1 = (f32[5,64,128]{2,1,0:T(8,128)S(1)}, f32[8,4,64,128]{3,2,1,0:T(8,128)}) custom-call(f32[5,64,128]{2,1,0:T(8,128)S(1)} %collective-permute-done.from_ref, f32[8,4,64,128]{3,2,1,0:T(8,128)} %get-tuple-element.12.base_ref, f32[2080,128]{1,0:T(8,128)S(1)} %bitcast.5, ...), custom_call_target="tpu_custom_call", output_to_operand_aliasing={{1}: (1, {})} | custom-call | tf_op jit(solution)/shard_map/relay/pallas_call | solution.py:244
  56.8 0.7 %collective-permute-start.2 = (f32[5,64,128]{2,1,0:T(8,128)S(1)}, f32[5,64,128]{2,1,0:T(8,128)S(1)}, u32[]{:S(2)}, u32[]{:S(2)}) collective-permute-start(f32[5,64,128]{2,1,0:T(8,128)S(1)} %get-tuple-element.16), channel_id=1, source_target_pairs={{3,2},{5,4},{7,6},{11,10},{13,12},{15,14},{19,18},{21,20},{23,22},... | collective-permute-start | bytes 491528 | tf_op jit(solution)/shard_map/ppermute | solution.py:254
  57.5 1.8 %collective-permute-done.3.above_ref = f32[5,64,128]{2,1,0:T(8,128)S(1)} collective-permute-done((f32[5,64,128]{2,1,0:T(8,128)S(1)}, f32[5,64,128]{2,1,0:T(8,128)S(1)}, u32[]{:S(2)}, u32[]{:S(2)}) %collective-permute-start.3) | collective-permute-done | bytes 163872 | tf_op jit(solution)/shard_map/ppermute | solution.py:225
  59.3 0.0 collective-permute-done.2.below_ref
  59.3 0.7 %finish.1 = f32[8,4,64,128]{3,2,1,0:T(8,128)} custom-call(f32[8,4,64,128]{3,2,1,0:T(8,128)} %get-tuple-element.15.base_ref, f32[2080,128]{1,0:T(8,128)S(1)} %bitcast.6, f32[5,2,64,128]{3,2,1,0:T(8,128)S(1)} %get-tuple-element.13.part_ref, f32[5,64,128]{2,1,0:T(8,128)S(1)} %collective-permute-done.2.below_ref, ...), custom_call_target="tpu_custom_call", output_to_operand_aliasing={{}: (0, {})} | custom-call | tf_op jit(solution)/shard_map/finish/pallas_call | solution.py:255
  (1 shorter events, 0.0 us)
Async XLA Ops:
  0.0 26.1 %copy-start.1 = (f32[4]{0:T(128)S(1)}, f32[4]{0:T(128)}, u32[]{:S(2)}) copy-start(f32[4]{0:T(128)} %fracs_ref.1) | copy-start | bytes 52
  0.0 26.1 %copy-start = (s32[4]{0:T(128)S(1)}, s32[4]{0:T(128)}, u32[]{:S(2)}) copy-start(s32[4]{0:T(128)} %shifts_ref.1) | copy-start | bytes 52
  47.6 11.7 %collective-permute-start.3 = (f32[5,64,128]{2,1,0:T(8,128)S(1)}, f32[5,64,128]{2,1,0:T(8,128)S(1)}, u32[]{:S(2)}, u32[]{:S(2)}) collective-permute-start(f32[5,64,128]{2,1,0:T(8,128)S(1)} %get-tuple-element.11), channel_id=1, source_target_pairs={{2,1},{4,3},{6,5},{10,9},{12,11},{14,13},{18,17},{20,19},{22,21},{... | collective-permute-start | bytes 491528 | tf_op jit(solution)/shard_map/ppermute | solution.py:225
  48.9 7.2 %collective-permute-start = (f32[5,64,128]{2,1,0:T(8,128)S(1)}, f32[5,64,128]{2,1,0:T(8,128)S(1)}, u32[]{:S(2)}, u32[]{:S(2)}) collective-permute-start(f32[5,64,128]{2,1,0:T(8,128)S(1)} %get-tuple-element.11), channel_id=1, source_target_pairs={{1,3},{3,5},{5,7},{9,11},{11,13},{13,15},{17,19},{19,21},{21,23},{... | collective-permute-start | bytes 491528 | tf_op jit(solution)/shard_map/ppermute | solution.py:224
  53.8 1.6 %collective-permute-start.1 = (f32[5,64,128]{2,1,0:T(8,128)S(1)}, f32[5,64,128]{2,1,0:T(8,128)S(1)}, u32[]{:S(2)}, u32[]{:S(2)}) collective-permute-start(f32[5,64,128]{2,1,0:T(8,128)S(1)} %get-tuple-element.14), channel_id=1, source_target_pairs={{0,1},{1,0},{2,3},{3,2},{4,5},{5,4},{6,7},{7,6},{8,9},{9,8},{10,11... | collective-permute-start | bytes 491528 | tf_op jit(solution)/shard_map/ppermute | solution.py:226
  56.8 2.5 %collective-permute-start.2 = (f32[5,64,128]{2,1,0:T(8,128)S(1)}, f32[5,64,128]{2,1,0:T(8,128)S(1)}, u32[]{:S(2)}, u32[]{:S(2)}) collective-permute-start(f32[5,64,128]{2,1,0:T(8,128)S(1)} %get-tuple-element.16), channel_id=1, source_target_pairs={{3,2},{5,4},{7,6},{11,10},{13,12},{15,14},{19,18},{21,20},{23,22},... | collective-permute-start | bytes 491528 | tf_op jit(solution)/shard_map/ppermute | solution.py:254

commit v9 on v7

--- a/solution.py
+++ b/solution.py
@@ -19,7 +19,7 @@
 EDGE_SETTLED = (2, 3, 4)
 
 
-def remap_kernel(shifts_ref, fracs_ref, x_ref, o_ref, ends_ref):
+def remap_kernel(shifts_ref, fracs_ref, x_ref, o_ref):
     blocks, height, width = x_ref.shape
     tall = height + 1
     mine = lax.rem(lax.axis_index("az"), shifts_ref.shape[0])
@@ -42,15 +42,13 @@
     for i in range(blocks):
         cells = o_ref[tall * i : tall * i + height, :]
         ends = jnp.where(pair == i, pltpu.roll(cells, (2 * i + 1) % width, 1), ends)
-    rows = jnp.transpose(jnp.concatenate([ends, jnp.zeros((width - height, width), F32)], axis=0))
-    used = 2 * blocks
-    ends_ref[0] = rows[:used]
-    ends_ref[1] = pltpu.roll(rows[:used], height, 1)
+    tip = 2 * (blocks - 1)
+    before = jnp.where(lane == 0, pltpu.roll(ends, width - tip, 1), pltpu.roll(ends, 2, 1))
+    after = jnp.where(lane == tip, pltpu.roll(ends, tip - 1, 1), pltpu.roll(ends, width - 3, 1))
+    rows = jnp.transpose(jnp.concatenate([before, after], axis=0))
     for i in range(blocks):
-        last = 2 * ((i - 1) % blocks)
-        head = 2 * ((i + 1) % blocks) + 1
         at = tall * i + height
-        o_ref[at : at + 1, :] = ends_ref[0, last : last + 1, :] + ends_ref[1, head : head + 1, :]
+        o_ref[at : at + 1, :] = rows[2 * i : 2 * i + 1]
 
 
 def slab(s_ref, at, height):
@@ -201,7 +199,6 @@
         out_shape=jax.ShapeDtypeStruct((count * (height + 1), width), F32),
         in_specs=[SMEM, SMEM, VMEM],
         out_specs=VMEM,
-        scratch_shapes=[pltpu.VMEM((2, 2 * count, width), F32)],
         compiler_params=GRANT,
         name="remap",
     )(shifts, fracs, turned)

time: 60.3 us -> 60.3 us (level)
  no operation moved by 1% of the time
where the time goes in v9:
time: 60.3 us; the launch traced here: 60 us
  blocking collectives  45.9 us (76%)
  starting transfers between devices  6.96 us (12%)
  Pallas kernels  3.92 us (7%)
  waiting for transfers between devices  3.15 us (5%)
    all_to_all x1, blocking collectives, on_device(): lax.all_to_all(state.reshape(count, height, width), 'az', 0, 0, tiled=True)  26.1 us
    all_to_all x1, blocking collectives, on_device(): lax.all_to_all(moved, 'az', 0, 0, tiled=True)  19.9 us
    ppermute x1, starting transfers between devices, on_device(): relayed = lax.ppermute(far, 'rad', [(i, i + 2) for i in odd])  4.9 us
    ppermute x1, waiting for transfers between devices, on_device(): above = lax.ppermute(far, 'rad', [(i + 1, i) for i in odd])  2.46 us
    pallas_call x1, Pallas kernels, on_device(): pl.pallas_call(remap_kernel, out_shape=jax.ShapeDtypeStruct((count * (hei...  1.57 us
    pallas_call x1, Pallas kernels, on_device(): pl.pallas_call(main_kernel, out_shape=(whole, jax.ShapeDtypeStruct((chang...  1.51 us
    ppermute x1, starting transfers between devices, on_device(): above = lax.ppermute(far, 'rad', [(i + 1, i) for i in odd])  1.29 us
  transfers between devices with their start and end apart: 4, of which 2 were waited for; matrix products, arithmetic and copies ran while one was open for 0% of the time, Pallas kernels for 3%

profile of v9, /device:TPU:1, one launch (start us, length us, event | category | flops | bytes accessed | tf_op | source)
XLA Modules:
  0.0 60.0 jit_solution(12032085266210895995)
XLA Ops:
  0.0 0.0 copy-start.1
  0.0 0.0 copy-start
  0.0 26.1 %all_to_all.10.x_ref = f32[32,64,128]{2,1,0:T(8,128)S(1)} all-to-all(f32[32,64,128]{2,1,0:T(8,128)} %bitcast.7), channel_id=1, replica_groups=mesh['az'=32,'rad'=8] {'az'}, dimensions={0} | all-to-all | bytes 2097152 | tf_op jit(solution)/shard_map/all_to_all | solution.py:196
  26.1 0.0 copy-done.1
  26.1 0.0 copy-done
  26.1 1.6 %remap.1 = f32[2080,128]{1,0:T(8,128)S(1)} custom-call(s32[4]{0:T(128)S(1)} %copy-done, f32[4]{0:T(128)S(1)} %copy-done.1, f32[32,64,128]{2,1,0:T(8,128)S(1)} %all_to_all.10.x_ref), custom_call_target="tpu_custom_call" | custom-call | tf_op jit(solution)/shard_map/remap/pallas_call | solution.py:197
  27.7 19.9 %all_to_all.11 = f32[32,65,1,128]{3,2,1,0:T(1,128)S(1)} all-to-all(f32[32,65,1,128]{3,2,1,0:T(1,128)S(1)} %bitcast.6), channel_id=1, replica_groups=mesh['az'=32,'rad'=8] {'az'}, dimensions={0} | all-to-all | bytes 2129920 | tf_op jit(solution)/shard_map/all_to_all | solution.py:206
  47.6 1.3 %collective-permute-start.3 = (f32[5,64,128]{2,1,0:T(8,128)S(1)}, f32[5,64,128]{2,1,0:T(8,128)S(1)}, u32[]{:S(2)}, u32[]{:S(2)}) collective-permute-start(f32[5,64,128]{2,1,0:T(8,128)S(1)} %get-tuple-element.11), channel_id=1, source_target_pairs={{2,1},{4,3},{6,5},{10,9},{12,11},{14,13},{18,17},{20,19},{22,21},{... | collective-permute-start | bytes 491528 | tf_op jit(solution)/shard_map/ppermute | solution.py:218
  48.9 4.9 %collective-permute-start = (f32[5,64,128]{2,1,0:T(8,128)S(1)}, f32[5,64,128]{2,1,0:T(8,128)S(1)}, u32[]{:S(2)}, u32[]{:S(2)}) collective-permute-start(f32[5,64,128]{2,1,0:T(8,128)S(1)} %get-tuple-element.11), channel_id=1, source_target_pairs={{1,3},{3,5},{5,7},{9,11},{11,13},{13,15},{17,19},{19,21},{21,23},{... | collective-permute-start | bytes 491528 | tf_op jit(solution)/shard_map/ppermute | solution.py:217
  53.8 1.5 %main.1 = (f32[8,4,64,128]{3,2,1,0:T(8,128)}, f32[5,2,64,128]{3,2,1,0:T(8,128)S(1)}) custom-call(f32[2080,128]{1,0:T(8,128)S(1)} %bitcast.4), custom_call_target="tpu_custom_call" | custom-call | flops 4000000000 | bytes 4194304 | tf_op jit(solution)/shard_map/main/pallas_call | solution.py:222
  55.3 0.1 collective-permute-start.2
  55.4 0.7 %collective-permute-done.from_ref = f32[5,64,128]{2,1,0:T(8,128)S(1)} collective-permute-done((f32[5,64,128]{2,1,0:T(8,128)S(1)}, f32[5,64,128]{2,1,0:T(8,128)S(1)}, u32[]{:S(2)}, u32[]{:S(2)}) %collective-permute-start) | collective-permute-done | bytes 163872 | tf_op jit(solution)/shard_map/ppermute | solution.py:217
  56.1 0.7 %collective-permute-start.1 = (f32[5,64,128]{2,1,0:T(8,128)S(1)}, f32[5,64,128]{2,1,0:T(8,128)S(1)}, u32[]{:S(2)}, u32[]{:S(2)}) collective-permute-start(f32[5,64,128]{2,1,0:T(8,128)S(1)} %relay.1), channel_id=1, source_target_pairs={{3,2},{5,4},{7,6},{11,10},{13,12},{15,14},{19,18},{21,20},{23,22},... | collective-permute-start | bytes 491528 | tf_op jit(solution)/shard_map/ppermute | solution.py:244
  56.8 0.0 collective-permute-done.2.chip_ref
  56.8 2.5 %collective-permute-done.3.above_ref = f32[5,64,128]{2,1,0:T(8,128)S(1)} collective-permute-done((f32[5,64,128]{2,1,0:T(8,128)S(1)}, f32[5,64,128]{2,1,0:T(8,128)S(1)}, u32[]{:S(2)}, u32[]{:S(2)}) %collective-permute-start.3) | collective-permute-done | bytes 163872 | tf_op jit(solution)/shard_map/ppermute | solution.py:218
  59.3 0.0 collective-permute-done.1.below_ref
  59.3 0.8 %finish.1 = f32[8,4,64,128]{3,2,1,0:T(8,128)} custom-call(f32[8,4,64,128]{3,2,1,0:T(8,128)} %get-tuple-element.9.base_ref, f32[2080,128]{1,0:T(8,128)S(1)} %bitcast.5, f32[5,2,64,128]{3,2,1,0:T(8,128)S(1)} %get-tuple-element.10.part_ref, f32[5,64,128]{2,1,0:T(8,128)S(1)} %collective-permute-done.1.below_ref, ...), custom_call_target="tpu_custom_call", output_to_operand_aliasing={{}: (0, {})} | custom-call | tf_op jit(solution)/shard_map/finish/pallas_call | solution.py:245
  (2 shorter events, 0.1 us)
Async XLA Ops:
  0.0 26.1 %copy-start.1 = (f32[4]{0:T(128)S(1)}, f32[4]{0:T(128)}, u32[]{:S(2)}) copy-start(f32[4]{0:T(128)} %fracs_ref.1) | copy-start | bytes 52
  0.0 26.1 %copy-start = (s32[4]{0:T(128)S(1)}, s32[4]{0:T(128)}, u32[]{:S(2)}) copy-start(s32[4]{0:T(128)} %shifts_ref.1) | copy-start | bytes 52
  47.6 11.7 %collective-permute-start.3 = (f32[5,64,128]{2,1,0:T(8,128)S(1)}, f32[5,64,128]{2,1,0:T(8,128)S(1)}, u32[]{:S(2)}, u32[]{:S(2)}) collective-permute-start(f32[5,64,128]{2,1,0:T(8,128)S(1)} %get-tuple-element.11), channel_id=1, source_target_pairs={{2,1},{4,3},{6,5},{10,9},{12,11},{14,13},{18,17},{20,19},{22,21},{... | collective-permute-start | bytes 491528 | tf_op jit(solution)/shard_map/ppermute | solution.py:218
  48.9 7.2 %collective-permute-start = (f32[5,64,128]{2,1,0:T(8,128)S(1)}, f32[5,64,128]{2,1,0:T(8,128)S(1)}, u32[]{:S(2)}, u32[]{:S(2)}) collective-permute-start(f32[5,64,128]{2,1,0:T(8,128)S(1)} %get-tuple-element.11), channel_id=1, source_target_pairs={{1,3},{3,5},{5,7},{9,11},{11,13},{13,15},{17,19},{19,21},{21,23},{... | collective-permute-start | bytes 491528 | tf_op jit(solution)/shard_map/ppermute | solution.py:217
  55.3 1.5 %collective-permute-start.2 = (f32[5,64,128]{2,1,0:T(8,128)S(1)}, f32[5,64,128]{2,1,0:T(8,128)S(1)}, u32[]{:S(2)}, u32[]{:S(2)}) collective-permute-start(f32[5,64,128]{2,1,0:T(8,128)S(1)} %get-tuple-element.12), channel_id=1, source_target_pairs={{0,1},{1,0},{2,3},{3,2},{4,5},{5,4},{6,7},{7,6},{8,9},{9,8},{10,11... | collective-permute-start | bytes 491528 | tf_op jit(solution)/shard_map/ppermute | solution.py:219
  56.1 3.2 %collective-permute-start.1 = (f32[5,64,128]{2,1,0:T(8,128)S(1)}, f32[5,64,128]{2,1,0:T(8,128)S(1)}, u32[]{:S(2)}, u32[]{:S(2)}) collective-permute-start(f32[5,64,128]{2,1,0:T(8,128)S(1)} %relay.1), channel_id=1, source_target_pairs={{3,2},{5,4},{7,6},{11,10},{13,12},{15,14},{19,18},{21,20},{23,22},... | collective-permute-start | bytes 491528 | tf_op jit(solution)/shard_map/ppermute | solution.py:244
